TPU v7x, 512 devices: a whole 4x8x8 slice. The times are simulated.
512 devices in a mesh: space: 32 (over y, z_lo), replica: 16 (over z_hi, x, core).
Axes of the slice: x: 4, y: 8, z: 8 (z_hi: 2, z_lo: 4; z = z_hi * 4 + z_lo), core: 2. Of those that a mesh axis runs over, the one named last changes fastest.
Arguments:
- volumes: bfloat16 [16, 32, 2, 8, 16, 256], P('replica', 'space'), may hold values from -6 to 6
- weights: bfloat16 [3, 3, 3, 256, 128], replicated, may hold values from -0.078125 to 0.078125
- out_grads: bfloat16 [16, 32, 2, 8, 16, 128], P('replica', 'space'), may hold values from -6 to 6
Outputs:
- outputs: bfloat16 [16, 32, 2, 8, 16, 128], P('replica', 'space')
- in_grads: bfloat16 [16, 32, 2, 8, 16, 256], P('replica', 'space')
- kernel_grad: float32 [3, 3, 3, 256, 128], P(None, None, None, 'replica')
All inputs are finite; a program needn't handle non-finite values.
Results may differ from a plain program's by a relative error of at most 0.001.
Values may be sent and summed in bfloat16 or wider, within the bound.
A program may use at most 64 MiB of HBM per device.

v0:
```python
import jax
import jax.numpy as jnp
from jax import lax
from jax.sharding import PartitionSpec as P


def shifted(block, axis, distance):
    devices = range(lax.axis_size(axis))
    route = [(i - distance, i) for i in devices if i - distance in devices]
    return lax.ppermute(block, axis, route)


def windows(padded, row_tap, col_tap):
    size_x = padded.shape[0] - 2
    size_y = padded.shape[1] - 2
    size_z = padded.shape[2] - 2
    parts = [
        padded[row_tap : row_tap + size_x, col_tap : col_tap + size_y, depth : depth + size_z]
        for depth in range(3)
    ]
    joined = jnp.concatenate(parts, axis=-1)
    return joined.reshape(size_x * size_y * size_z, 3 * padded.shape[3])


def convolve(padded, kernel):
    chans_in = kernel.shape[3]
    chans_out = kernel.shape[4]
    shape_out = (padded.shape[0] - 2, padded.shape[1] - 2, padded.shape[2] - 2, chans_out)
    total = jnp.zeros((shape_out[0] * shape_out[1] * shape_out[2], chans_out), jnp.float32)
    for row_tap in range(3):
        for col_tap in range(3):
            window = windows(padded, row_tap, col_tap)
            total = total + jnp.dot(
                window,
                kernel[row_tap, col_tap].reshape(3 * chans_in, chans_out),
                preferred_element_type=jnp.float32,
            )
    return total.reshape(shape_out)


def kernel_terms(padded, grads):
    chans_in = padded.shape[3]
    flat_grads = grads.reshape(-1, grads.shape[-1])
    rows = []
    for row_tap in range(3):
        cols = []
        for col_tap in range(3):
            window = windows(padded, row_tap, col_tap)
            term = lax.dot_general(
                window, flat_grads, (((0,), (0,)), ((), ())), preferred_element_type=jnp.float32
            )
            cols.append(term.reshape(3, chans_in, flat_grads.shape[1]))
        rows.append(jnp.stack(cols, axis=0))
    return jnp.stack(rows, axis=0)


def extend(field, dim, stride, coord, count):
    length = field.shape[dim]
    last_layer = lax.slice_in_dim(field, length - 1, length, axis=dim)
    first_layer = lax.slice_in_dim(field, 0, 1, axis=dim)
    from_below = shifted(last_layer, "space", stride)
    from_above = shifted(first_layer, "space", -stride)
    from_below = jnp.where(coord > 0, from_below, jnp.zeros_like(from_below))
    from_above = jnp.where(coord < count - 1, from_above, jnp.zeros_like(from_above))
    return jnp.concatenate([from_below, field, from_above], axis=dim)


def per_device(volumes, weights, out_grads):
    blocks = volumes[0, 0]
    grads = out_grads[0, 0]
    place = lax.axis_index("space")
    grid_x = lax.axis_size("space") // 8
    layout = ((2, 1, place % 2, 2), (1, 2, place // 2 % 4, 4), (0, 8, place // 8, grid_x))

    def surround(field):
        for dim, stride, coord, count in layout:
            field = extend(field, dim, stride, coord, count)
        return field

    padded = surround(blocks)
    result = convolve(padded, weights).astype(jnp.bfloat16)
    partial_terms = kernel_terms(padded, grads)
    summed = lax.psum(partial_terms, "space")
    share = lax.psum_scatter(summed, "replica", scatter_dimension=3, tiled=True)
    cells_all = (
        lax.axis_size("space")
        * lax.axis_size("replica")
        * blocks.shape[0]
        * blocks.shape[1]
        * blocks.shape[2]
    )
    kernel_grad = share / jnp.sqrt(jnp.float32(cells_all))
    grad_padded = surround(grads)
    flipped = jnp.flip(weights, axis=(0, 1, 2)).transpose(0, 1, 2, 4, 3)
    back = convolve(grad_padded, flipped).astype(jnp.bfloat16)
    return (result[None, None], back[None, None], kernel_grad)


def solution(mesh):
    in_specs = (
        P("replica", "space", None, None, None, None),
        P(),
        P("replica", "space", None, None, None, None),
    )
    out_specs = (
        P("replica", "space", None, None, None, None),
        P("replica", "space", None, None, None, None),
        P(None, None, None, "replica", None),
    )
    return jax.shard_map(
        per_device, mesh=mesh, in_specs=in_specs, out_specs=out_specs, check_vma=False
    )
```

profile of v0, /device:TPU:2, one launch (start us, length us, event | category | flops | bytes accessed | tf_op | source)
XLA Modules:
  0.0 525.6 jit_solution(7983868832378239965)
XLA Ops:
  7.2 1.5 fusion.17
  8.7 1.3 collective-permute-start.1
  10.0 5.5 %collective-permute-start = (bf16[2,8,1,256]{3,2,1,0:T(2,128)(2,1)}, bf16[2,8,1,256]{3,2,1,0:T(2,128)(2,1)}, u32[]{:S(2)}, u32[]{:S(2)}) collective-permute-start(bf16[2,8,1,256]{3,2,1,0:T(2,128)(2,1)} %get-tuple-element.73), channel_id=1, source_target_pairs={{0,16},{16,32},{32,48},{48,64},{64,80},{80,96},{96,112},{112,128},... | collective-permute-start | bytes 24584 | tf_op jit(solution)/shard_map/ppermute | solution.py:10
  15.5 1.4 fusion.21
  16.9 1.3 collective-permute-start.7
  18.2 5.3 %collective-permute-start.6 = (bf16[2,8,1,128]{3,2,1,0:T(2,128)(2,1)}, bf16[2,8,1,128]{3,2,1,0:T(2,128)(2,1)}, u32[]{:S(2)}, u32[]{:S(2)}) collective-permute-start(bf16[2,8,1,128]{3,2,1,0:T(2,128)(2,1)} %get-tuple-element.91), channel_id=1, source_target_pairs={{0,16},{16,32},{32,48},{48,64},{64,80},{80,96},{96,112},{112,128},... | collective-permute-start | bytes 12296 | tf_op jit(solution)/shard_map/ppermute | solution.py:10
  23.5 2.7 fusion.9
  26.2 0.9 copy.20
  27.2 1.3 fusion.8
  28.7 0.7 pad_maximum_fusion.27
  29.5 1.3 collective-permute-start.9
  30.8 8.3 %collective-permute-start.8 = (bf16[2,1,18,128]{3,2,1,0:T(8,128)(2,1)S(1)}, bf16[2,1,18,128]{3,2,1,0:T(8,128)(2,1)S(1)}, u32[]{:S(2)}, u32[]{:S(2)}) collective-permute-start(bf16[2,1,18,128]{3,2,1,0:T(8,128)(2,1)S(1)} %get-tuple-element.87), channel_id=1, source_target_pairs={{0,32},{16,48},{32,64},{48,80},{64,96},{80,112},{96,128},{112,144}... | collective-permute-start | bytes 27656 | tf_op jit(solution)/shard_map/ppermute | solution.py:10
  39.0 0.7 broadcast_select_fusion.4
  40.0 1.3 collective-permute-start.3
  41.3 7.2 %collective-permute-start.2 = (bf16[2,1,18,256]{3,2,1,0:T(8,128)(2,1)S(1)}, bf16[2,1,18,256]{3,2,1,0:T(8,128)(2,1)S(1)}, u32[]{:S(2)}, u32[]{:S(2)}) collective-permute-start(bf16[2,1,18,256]{3,2,1,0:T(8,128)(2,1)S(1)} %get-tuple-element.69), channel_id=1, source_target_pairs={{0,32},{16,48},{32,64},{48,80},{64,96},{80,112},{96,128},{112,144}... | collective-permute-start | bytes 55304 | tf_op jit(solution)/shard_map/ppermute | solution.py:10
  48.7 0.2 convolution_bitcast_fusion.4
  49.2 0.7 fusion.18
  49.9 1.3 collective-permute-start.11
  51.2 7.6 %collective-permute-start.10 = (bf16[1,10,18,128]{3,2,1,0:T(8,128)(2,1)}, bf16[1,10,18,128]{3,2,1,0:T(8,128)(2,1)}, u32[]{:S(2)}, u32[]{:S(2)}) collective-permute-start(bf16[1,10,18,128]{3,2,1,0:T(8,128)(2,1)} %get-tuple-element.76), channel_id=1, source_target_pairs={{0,128},{16,144},{32,160},{48,176},{64,192},{80,208},{96,224},{112... | collective-permute-start | bytes 138248 | tf_op jit(solution)/shard_map/ppermute | solution.py:10
  58.9 0.7 pad_maximum_fusion.16
  59.6 0.7 pad_maximum_fusion.17
  60.6 0.7 fusion.12
  61.3 1.3 collective-permute-start.5
  62.6 8.8 %collective-permute-start.4 = (bf16[1,10,18,256]{3,2,1,0:T(8,128)(2,1)}, bf16[1,10,18,256]{3,2,1,0:T(8,128)(2,1)}, u32[]{:S(2)}, u32[]{:S(2)}) collective-permute-start(bf16[1,10,18,256]{3,2,1,0:T(8,128)(2,1)} %get-tuple-element.40), channel_id=1, source_target_pairs={{0,128},{16,144},{32,160},{48,176},{64,192},{80,208},{96,224},{112... | collective-permute-start | bytes 276488 | tf_op jit(solution)/shard_map/ppermute | solution.py:10
  71.8 0.2 convolution_bitcast_fusion.3
  72.3 0.3 convolution_bitcast_fusion.5
  72.7 1.5 broadcast_select_fusion.2
  74.1 0.9 broadcast_select_fusion
  75.3 1.2 fusion.10
  76.7 1.0 convolution_bitcast_fusion
  77.9 1.0 convolution_bitcast_fusion.1
  78.9 1.1 pad_maximum_fusion.7
  80.0 0.9 copy.26
  80.9 2.0 convolution_bitcast_fusion.2
  82.9 1.8 pad_maximum_fusion.3
  84.7 1.9 copy.23
  86.7 2.0 convolution_bitcast_fusion.6
  88.7 1.8 pad_maximum_fusion.2
  90.5 1.9 copy.22
  92.4 2.0 convolution_bitcast_fusion.7
  94.4 1.8 pad_maximum_fusion.1
  96.2 1.9 copy.21
  98.1 1.2 convolution_bitcast_fusion.8
  99.3 1.4 maximum_bitcast_fusion.2
  100.9 2.0 pad_maximum_fusion
  103.0 0.7 copy-done.34
  104.3 0.7 copy-done.19
  105.2 0.2 convolution_add_fusion.7
  105.5 0.2 convolution_add_fusion.6
  106.3 0.2 convolution_add_fusion.4
  106.8 0.2 copy-done.8
  107.5 0.9 fusion
  108.4 0.2 fusion.22
  108.7 0.2 convolution_add_fusion.15
  109.0 0.3 convolution_add_fusion.14
  109.4 0.2 convolution_add_fusion.13
  109.8 0.3 convolution_add_fusion.12
  110.3 0.2 convolution_add_fusion.11
  110.6 0.2 convolution_add_fusion.10
  111.1 0.2 convolution_add_fusion.9
  111.3 108.3 %reduce-scatter.2.cloned.1.call-done = f32[3,3,3,16,128]{4,3,2,1,0:T(8,128)} async-done(((f32[3,3,3,256,128]{4,3,2,1,0:T(8,128)}), f32[3,3,3,16,128]{4,3,2,1,0:T(8,128)}) %reduce-scatter.2.cloned.1.call-update) | async-done | bytes 221200 | tf_op jit(solution)/shard_map/reduce_scatter | solution.py:84
  219.7 0.9 fusion.1
  220.6 296.5 %all-reduce.2.cloned.1.call-done = f32[3,3,3,16,128]{4,3,2,1,0:T(8,128)} async-done(((f32[3,3,3,16,128]{4,3,2,1,0:T(8,128)}), f32[3,3,3,16,128]{4,3,2,1,0:T(8,128)}) %all-reduce.2.cloned.1.call-update) | async-done | bytes 221200 | tf_op jit(solution)/shard_map/psum | solution.py:83
  517.1 1.6 broadcast_multiply_fusion
  (140 shorter events, 5.4 us)
Async XLA Ops:
  7.2 212.5 %reduce-scatter.2.cloned.1.call-start = ((), (), s32[]{:S(2)}) async-start(), calls=%async_computation.1 | async-start | bytes 3760128 | tf_op jit(solution)/shard_map/reduce_scatter | solution.py:84
  8.7 30.3 %collective-permute-start.1 = (bf16[2,8,1,256]{3,2,1,0:T(2,128)(2,1)}, bf16[2,8,1,256]{3,2,1,0:T(2,128)(2,1)}, u32[]{:S(2)}, u32[]{:S(2)}) collective-permute-start(bf16[2,8,1,256]{3,2,1,0:T(2,128)(2,1)} %get-tuple-element.74), channel_id=1, source_target_pairs={{16,0},{32,16},{48,32},{64,48},{80,64},{96,80},{112,96},{128,112},... | collective-permute-start | bytes 24584 | tf_op jit(solution)/shard_map/ppermute | solution.py:10
  10.0 29.8 %collective-permute-start = (bf16[2,8,1,256]{3,2,1,0:T(2,128)(2,1)}, bf16[2,8,1,256]{3,2,1,0:T(2,128)(2,1)}, u32[]{:S(2)}, u32[]{:S(2)}) collective-permute-start(bf16[2,8,1,256]{3,2,1,0:T(2,128)(2,1)} %get-tuple-element.73), channel_id=1, source_target_pairs={{0,16},{16,32},{32,48},{48,64},{64,80},{80,96},{96,112},{112,128},... | collective-permute-start | bytes 24584 | tf_op jit(solution)/shard_map/ppermute | solution.py:10
  16.9 11.7 %collective-permute-start.7 = (bf16[2,8,1,128]{3,2,1,0:T(2,128)(2,1)S(1)}, bf16[2,8,1,128]{3,2,1,0:T(2,128)(2,1)S(1)}, u32[]{:S(2)}, u32[]{:S(2)}) collective-permute-start(bf16[2,8,1,128]{3,2,1,0:T(2,128)(2,1)S(1)} %get-tuple-element.92), channel_id=1, source_target_pairs={{16,0},{32,16},{48,32},{64,48},{80,64},{96,80},{112,96},{128,112},... | collective-permute-start | bytes 12296 | tf_op jit(solution)/shard_map/ppermute | solution.py:10
  18.2 8.0 %copy-start.1 = (bf16[3,3,3,256,128]{4,3,2,1,0:T(8,128)(2,1)S(1)}, bf16[3,3,3,256,128]{4,3,2,1,0:T(8,128)(2,1)}, u32[]{:S(2)}) copy-start(bf16[3,3,3,256,128]{4,3,2,1,0:T(8,128)(2,1)} %param.4) | copy-start | bytes 5308420
  18.2 10.5 %collective-permute-start.6 = (bf16[2,8,1,128]{3,2,1,0:T(2,128)(2,1)}, bf16[2,8,1,128]{3,2,1,0:T(2,128)(2,1)}, u32[]{:S(2)}, u32[]{:S(2)}) collective-permute-start(bf16[2,8,1,128]{3,2,1,0:T(2,128)(2,1)} %get-tuple-element.91), channel_id=1, source_target_pairs={{0,16},{16,32},{32,48},{48,64},{64,80},{80,96},{96,112},{112,128},... | collective-permute-start | bytes 12296 | tf_op jit(solution)/shard_map/ppermute | solution.py:10
  27.2 1.3 copy-start.2
  27.2 1.5 copy-start
  28.6 20.1 %copy-start.26 = (bf16[256,256]{0,1:T(8,128)(2,1)}, bf16[256,256]{0,1:T(8,128)(2,1)S(1)}, u32[]{:S(2)}) copy-start(bf16[256,256]{0,1:T(8,128)(2,1)S(1)} %copy.18) | copy-start | bytes 393220
  29.5 19.5 %collective-permute-start.9 = (bf16[2,1,18,128]{3,2,1,0:T(8,128)(2,1)S(1)}, bf16[2,1,18,128]{3,2,1,0:T(8,128)(2,1)S(1)}, u32[]{:S(2)}, u32[]{:S(2)}) collective-permute-start(bf16[2,1,18,128]{3,2,1,0:T(8,128)(2,1)S(1)} %get-tuple-element.88), channel_id=1, source_target_pairs={{32,0},{48,16},{64,32},{80,48},{96,64},{112,80},{128,96},{144,112}... | collective-permute-start | bytes 27656 | tf_op jit(solution)/shard_map/ppermute | solution.py:10
  30.8 18.3 %collective-permute-start.8 = (bf16[2,1,18,128]{3,2,1,0:T(8,128)(2,1)S(1)}, bf16[2,1,18,128]{3,2,1,0:T(8,128)(2,1)S(1)}, u32[]{:S(2)}, u32[]{:S(2)}) collective-permute-start(bf16[2,1,18,128]{3,2,1,0:T(8,128)(2,1)S(1)} %get-tuple-element.87), channel_id=1, source_target_pairs={{0,32},{16,48},{32,64},{48,80},{64,96},{80,112},{96,128},{112,144}... | collective-permute-start | bytes 27656 | tf_op jit(solution)/shard_map/ppermute | solution.py:10
  40.0 20.4 %collective-permute-start.3 = (bf16[2,1,18,256]{3,2,1,0:T(8,128)(2,1)S(1)}, bf16[2,1,18,256]{3,2,1,0:T(8,128)(2,1)S(1)}, u32[]{:S(2)}, u32[]{:S(2)}) collective-permute-start(bf16[2,1,18,256]{3,2,1,0:T(8,128)(2,1)S(1)} %get-tuple-element.70), channel_id=1, source_target_pairs={{32,0},{48,16},{64,32},{80,48},{96,64},{112,80},{128,96},{144,112}... | collective-permute-start | bytes 55304 | tf_op jit(solution)/shard_map/ppermute | solution.py:10
  41.3 19.1 %collective-permute-start.2 = (bf16[2,1,18,256]{3,2,1,0:T(8,128)(2,1)S(1)}, bf16[2,1,18,256]{3,2,1,0:T(8,128)(2,1)S(1)}, u32[]{:S(2)}, u32[]{:S(2)}) collective-permute-start(bf16[2,1,18,256]{3,2,1,0:T(8,128)(2,1)S(1)} %get-tuple-element.69), channel_id=1, source_target_pairs={{0,32},{16,48},{32,64},{48,80},{64,96},{80,112},{96,128},{112,144}... | collective-permute-start | bytes 55304 | tf_op jit(solution)/shard_map/ppermute | solution.py:10
  48.6 0.7 copy-start.28
  48.7 1.2 copy-start.30
  49.0 9.8 %copy-start.35 = (bf16[2,1,18,128]{3,2,1,0:T(8,128)(2,1)}, bf16[2,1,18,128]{3,2,1,0:T(8,128)(2,1)S(1)}, u32[]{:S(2)}) copy-start(bf16[2,1,18,128]{3,2,1,0:T(8,128)(2,1)S(1)} %broadcast_select_fusion.10) | copy-start | bytes 27652
  49.1 9.8 %copy-start.37 = (bf16[2,1,18,128]{3,2,1,0:T(8,128)(2,1)}, bf16[2,1,18,128]{3,2,1,0:T(8,128)(2,1)S(1)}, u32[]{:S(2)}) copy-start(bf16[2,1,18,128]{3,2,1,0:T(8,128)(2,1)S(1)} %broadcast_select_fusion.11) | copy-start | bytes 27652
  49.9 22.8 %collective-permute-start.11 = (bf16[1,10,18,128]{3,2,1,0:T(8,128)(2,1)}, bf16[1,10,18,128]{3,2,1,0:T(8,128)(2,1)}, u32[]{:S(2)}, u32[]{:S(2)}) collective-permute-start(bf16[1,10,18,128]{3,2,1,0:T(8,128)(2,1)} %get-tuple-element.75), channel_id=1, source_target_pairs={{128,0},{144,16},{160,32},{176,48},{192,64},{208,80},{224,96},{240... | collective-permute-start | bytes 138248 | tf_op jit(solution)/shard_map/ppermute | solution.py:10
  51.2 51.8 %collective-permute-start.10 = (bf16[1,10,18,128]{3,2,1,0:T(8,128)(2,1)}, bf16[1,10,18,128]{3,2,1,0:T(8,128)(2,1)}, u32[]{:S(2)}, u32[]{:S(2)}) collective-permute-start(bf16[1,10,18,128]{3,2,1,0:T(8,128)(2,1)} %get-tuple-element.76), channel_id=1, source_target_pairs={{0,128},{16,144},{32,160},{48,176},{64,192},{80,208},{96,224},{112... | collective-permute-start | bytes 138248 | tf_op jit(solution)/shard_map/ppermute | solution.py:10
  61.3 12.8 %collective-permute-start.5 = (bf16[1,10,18,256]{3,2,1,0:T(8,128)(2,1)}, bf16[1,10,18,256]{3,2,1,0:T(8,128)(2,1)}, u32[]{:S(2)}, u32[]{:S(2)}) collective-permute-start(bf16[1,10,18,256]{3,2,1,0:T(8,128)(2,1)} %get-tuple-element.39), channel_id=1, source_target_pairs={{128,0},{144,16},{160,32},{176,48},{192,64},{208,80},{224,96},{240... | collective-permute-start | bytes 276488 | tf_op jit(solution)/shard_map/ppermute | solution.py:10
  62.6 12.4 %collective-permute-start.4 = (bf16[1,10,18,256]{3,2,1,0:T(8,128)(2,1)}, bf16[1,10,18,256]{3,2,1,0:T(8,128)(2,1)}, u32[]{:S(2)}, u32[]{:S(2)}) collective-permute-start(bf16[1,10,18,256]{3,2,1,0:T(8,128)(2,1)} %get-tuple-element.40), channel_id=1, source_target_pairs={{0,128},{16,144},{32,160},{48,176},{64,192},{80,208},{96,224},{112... | collective-permute-start | bytes 276488 | tf_op jit(solution)/shard_map/ppermute | solution.py:10
  99.3 1.4 copy-start.6
  99.3 1.5 copy-start.7
  102.9 0.8 copy-start.34
  102.9 0.8 copy-start.36
  102.9 0.8 copy-start.38
  103.0 414.2 %all-reduce.2.cloned.1.call-start = ((), (), s32[]{:S(2)}) async-start(), calls=%async_computation.2 | async-start | bytes 442368 | tf_op jit(solution)/shard_map/psum | solution.py:83
  104.0 0.9 copy-start.19
  104.1 1.1 copy-start.13
  104.2 1.3 copy-start.12
  105.0 1.0 copy-start.11
  105.0 1.1 copy-start.15
  105.2 1.1 copy-start.10
  105.2 1.1 copy-start.32
  105.2 1.1 copy-start.33
  105.5 1.1 copy-start.9
  105.5 1.1 copy-start.14
  106.0 1.0 copy-start.8
  106.5 1.0 copy-start.18
  107.0 1.4 copy-start.5
  107.0 1.4 copy-start.17
  107.2 1.4 copy-start.4
  107.3 1.4 copy-start.25
  107.5 1.5 copy-start.3
  107.5 1.5 copy-start.24
  108.4 1.0 copy-start.23
  108.7 1.0 copy-start.27
  108.7 1.0 copy-start.29
  108.7 1.0 copy-start.31
  108.7 1.1 copy-start.39
  109.3 1.0 copy-start.22
  109.6 1.0 copy-start.21
  110.1 1.0 copy-start.20
  110.5 109.2 %copy-start.16 = (bf16[1,1,3,256,128]{4,3,2,1,0:T(8,128)(2,1)S(1)}, bf16[1,1,3,256,128]{4,3,2,1,0:T(8,128)(2,1)}, u32[]{:S(2)}) copy-start(bf16[1,1,3,256,128]{4,3,2,1,0:T(8,128)(2,1)} %get-tuple-element.12) | copy-start | bytes 589828
Sparse Core Ops, SparseCore 0:
  103.1 116.5 reduce-scatter.1
  222.6 294.5 all-reduce.1
where the time goes:
time: 527 us; the launch traced here: 526 us
  waiting for transfers between devices  405 us (77%)
  starting transfers between devices  50.5 us (10%)
  local copies, waits for them, and re-layouts  21.4 us (4%)
  other arithmetic  18.2 us (3%)
  matrix products  15.6 us (3%)
  between operations  15 us (3%)
    psum x1, waiting for transfers between devices, per_device(): summed = lax.psum(partial_terms, 'space')  297 us
    reduce_scatter x1, waiting for transfers between devices, per_device(): share = lax.psum_scatter(summed, 'replica', scatter_dimension=3, tiled=True)  108 us
    ppermute x12, starting transfers between devices, shifted(): return lax.ppermute(block, axis, route)  50.4 us
  transfers between devices with their start and end apart: 14, of which 2 were waited for; matrix products, arithmetic and copies ran while one was open for 9% of the time, Pallas kernels for 0%

commit v1 on v0

v1 whole, which is shorter than its diff:
```python
import jax
import jax.numpy as jnp
from jax import lax
from jax.experimental import pallas as pl
from jax.experimental.pallas import tpu as pltpu
from jax.sharding import PartitionSpec as P

MESH = pl.DeviceIdType.MESH
F32 = jnp.float32
BF16 = jnp.bfloat16
GROUPS = 7
LIFT = 32768.0
PLANE = [(ox, oy) for ox in (-1, 0, 1) for oy in (-1, 0, 1)]
SIDES = [o for o in PLANE if o != (0, 0)]


def encode(u, msg):
    n = u.shape[0]
    top = jnp.max(jnp.max(jnp.abs(u), axis=0), axis=0, keepdims=True)
    top = jnp.maximum(top, 1e-30).astype(BF16)
    v = u * (LIFT / top.astype(F32))
    v2 = v * v
    v4 = v2 * v2
    msg[pl.ds(0, n)] = ((v4 * v2) * (v * jnp.abs(v))).astype(BF16)
    msg[n] = jnp.broadcast_to(top.astype(F32), (16, 128)).astype(BF16)


def decode(msg, n):
    y = msg[pl.ds(0, n)].astype(F32)
    scale = msg[n].astype(F32) * (1.0 / LIFT)
    a = jnp.abs(y)
    t = lax.rsqrt(lax.rsqrt(a))
    u = jnp.where(a == 0.0, 0.0, t * lax.rsqrt(t))
    return jnp.where(y < 0.0, -u, u) * scale


def kernel(
    x_hbm, w_hbm, g_hbm, out_hbm, back_hbm, kg_hbm,
    wv, xc, gc, x3, g3, xface, gface, xfr, gfr, xt,
    part, sib_recv, x_send, x_recv, own, y_send, y_recv, z_own, z_send, z_recv, kg,
    acc_f, acc_b, out_v, back_v,
    in_sem, out_sem, halo_s, halo_r, sib_s, sib_r, xs_s, xs_r, ys_s, ys_r, zs_s, zs_r, ag_s, ag_r,
):
    s = lax.axis_index("space")
    r = lax.axis_index("replica")
    y, zl = s // 4, s % 4
    zh, x, c = r // 8, (r // 2) % 4, r % 2
    gx, gy, gz = s // 8, (s // 2) % 4, s % 2

    loads = [
        pltpu.make_async_copy(g_hbm, gc.at[pl.ds(1, 2), pl.ds(1, 8)], in_sem.at[0]),
        pltpu.make_async_copy(x_hbm, xc.at[pl.ds(1, 2), pl.ds(1, 8)], in_sem.at[1]),
        pltpu.make_async_copy(w_hbm, wv, in_sem.at[2]),
    ]
    for load in loads:
        load.start()
    for field in (gc, xc):
        z = jnp.zeros((1, 10, 16, field.shape[3]), BF16)
        field[pl.ds(0, 1)] = z
        field[pl.ds(3, 1)] = z
        z = jnp.zeros((2, 1, 16, field.shape[3]), BF16)
        field[pl.ds(1, 2), pl.ds(0, 1)] = z
        field[pl.ds(1, 2), pl.ds(9, 1)] = z
    gfr[...] = jnp.zeros_like(gfr)
    xfr[...] = jnp.zeros_like(xfr)

    def inside(ox, oy):
        return (gx + ox >= 0) & (gx + ox <= 3) & (gy + oy >= 0) & (gy + oy <= 3)

    def at(ox, oy, other):
        return ((gx + ox) * 8 + (gy + oy) * 2 + (1 - gz if other else gz), r)

    sibling = (s, r + 1 - 2 * c)
    x_peers = [(s, zh * 8 + ((x + d) % 4) * 2 + c) for d in (1, 2, 3)]
    y_peers = [(((y + d) % 8) * 4 + zl, r) for d in range(1, 8)]

    def z_peer(d):
        z_to = (zh * 4 + zl + d) % 8
        return (y * 4 + z_to % 4, (z_to // 4) * 8 + x * 2 + c)

    z_peers = [z_peer(d) for d in range(1, 8)]

    barrier = pltpu.get_barrier_semaphore()

    def greet(who):
        pl.semaphore_signal(barrier, inc=1, device_id=who, device_id_type=MESH)

    greet(sibling)
    for who in x_peers + y_peers + z_peers:
        greet(who)
    expected = 18
    for ox, oy in PLANE:
        here = inside(ox, oy)
        if (ox, oy) == (0, 0):
            greet(at(0, 0, True))
            expected = expected + 1
            continue

        @pl.when(here)
        def _(ox=ox, oy=oy):
            greet(at(ox, oy, False))
            greet(at(ox, oy, True))

        expected = expected + jnp.where(here, 2, 0)

    def cut(o, size):
        return (pl.ds(1, size), pl.ds(1, size)) if o == 0 else (
            (pl.ds(size, 1), pl.ds(0, 1)) if o == 1 else (pl.ds(1, 1), pl.ds(size + 1, 1)))

    def slab(field, k, ox, oy, base):
        (xs, xd), (ys, yd) = cut(ox, 2), cut(oy, 8)
        return pltpu.make_async_remote_copy(
            field.at[xs, ys], field.at[xd, yd], halo_s.at[base + k], halo_r.at[base + k],
            device_id=at(ox, oy, False), device_id_type=MESH)

    def face(src, dst, k, ox, oy, base):
        return pltpu.make_async_remote_copy(
            src, dst.at[1 - ox, 1 - oy], halo_s.at[base + k], halo_r.at[base + k],
            device_id=at(ox, oy, True), device_id_type=MESH)

    def halo(field, fsrc, fdst, base, do):
        for k, (ox, oy) in enumerate(SIDES):
            here = inside(-ox, -oy) if do == "recv" else inside(ox, oy)

            @pl.when(here)
            def _(k=k, ox=ox, oy=oy):
                one = slab(field, k, ox, oy, base)
                two = face(fsrc, fdst, 8 + k, ox, oy, base)
                if do == "start":
                    one.start()
                    two.start()
                elif do == "recv":
                    one.wait_recv()
                    two.wait_recv()
                else:
                    one.wait_send()
                    two.wait_send()
        own_face = face(fsrc, fdst, 16, 0, 0, base)
        {"start": own_face.start, "recv": own_face.wait_recv, "send": own_face.wait_send}[do]()

    rows = lax.broadcasted_iota(jnp.int32, (16, 256), 0)
    cols = lax.broadcasted_iota(jnp.int32, (16, 256), 1)
    pick = jnp.where(cols == rows * 16 + jnp.where(gz == 0, 15, 0), 1.0, 0.0).astype(BF16)

    def interior(field):
        return field[pl.ds(1, 2), pl.ds(1, 8)].reshape(256, field.shape[3])

    loads[0].wait()
    gface[...] = jnp.dot(pick, interior(gc), preferred_element_type=F32).astype(BF16)
    pl.semaphore_wait(barrier, expected)
    halo(gc, gface, gfr, 0, "start")
    loads[1].wait()
    xface[...] = jnp.dot(pick, interior(xc), preferred_element_type=F32).astype(BF16)
    halo(xc, xface, xfr, 17, "start")
    xt[...] = interior(xc).T

    def shift_all(field, received, shifted):
        ch = field.shape[3]
        shifted[1] = field[...]
        ri = lax.broadcasted_iota(jnp.int32, (160, 208), 0)
        ci = lax.broadcasted_iota(jnp.int32, (160, 208), 1)
        zi, yi = ri % 16, ri // 16
        for layer in range(4):
            ox = (0, 1, 1, 2)[layer]
            xrow = (8, 0, 8, 0)[layer]
            face_row = jnp.where(yi == 0, 160 + xrow + 7, jnp.where(yi == 9, 192 + xrow, 176 + xrow + yi - 1))
            low_col = jnp.where(zi > 0, ri - 1, jnp.where(gz == 1, face_row, -1))
            high_col = jnp.where(zi < 15, ri + 1, jnp.where(gz == 0, face_row, -1))
            low = jnp.where(ci == low_col, 1.0, 0.0).astype(BF16)
            high = jnp.where(ci == high_col, 1.0, 0.0).astype(BF16)
            cells = jnp.concatenate([field[layer].reshape(160, ch), received[ox].reshape(48, ch)], axis=0)
            shifted[0, layer] = jnp.dot(low, cells, preferred_element_type=F32).astype(BF16).reshape(10, 16, ch)
            shifted[2, layer] = jnp.dot(high, cells, preferred_element_type=F32).astype(BF16).reshape(10, 16, ch)

    def tap_of(t):
        t = jnp.minimum(t, 26)
        return t // 9, (t // 3) % 3, t % 3

    def g_window(t):
        dx, dy, dz = tap_of(t)
        return g3[2 - dz, pl.ds(2 - dx, 2), pl.ds(2 - dy, 8)].reshape(256, 128)

    def x_window(t):
        dx, dy, dz = tap_of(t)
        return x3[dz, pl.ds(dx, 2), pl.ds(dy, 8)].reshape(256, 256)

    halo(gc, gface, gfr, 0, "recv")
    shift_all(gc, gfr, g3)

    def to_sibling(g):
        return pltpu.make_async_remote_copy(
            part.at[g, :, :, :, 1 - c], sib_recv.at[g], sib_s.at[g], sib_r.at[g],
            device_id=sibling, device_id_type=MESH)

    def to_x(g, d):
        return pltpu.make_async_remote_copy(
            x_send.at[g, d - 1], x_recv.at[g, d - 1], xs_s.at[g, d - 1], xs_r.at[g, d - 1],
            device_id=x_peers[d - 1], device_id_type=MESH)

    def to_y(g):
        slot = (g - y + 8) % 8 - 1
        return pltpu.make_async_remote_copy(
            y_send.at[g], y_recv.at[slot], ys_s.at[g], ys_r.at[slot],
            device_id=(g * 4 + zl, r), device_id_type=MESH)

    def from_y(slot):
        return pltpu.make_async_remote_copy(
            y_send.at[0], y_recv.at[slot], ys_s.at[0], ys_r.at[slot],
            device_id=y_peers[0], device_id_type=MESH)

    def to_z(d):
        z_to = (zh * 4 + zl + d) % 8
        return pltpu.make_async_remote_copy(
            z_send.at[z_to // 4], z_recv.at[d - 1], zs_s.at[d - 1], zs_r.at[d - 1],
            device_id=z_peers[d - 1], device_id_type=MESH)

    def gather(d):
        return pltpu.make_async_remote_copy(
            kg.at[y], kg.at[y], ag_s.at[d - 1], ag_r.at[y],
            device_id=y_peers[d - 1], device_id_type=MESH)

    def gathered(g):
        return pltpu.make_async_remote_copy(
            kg.at[g], kg.at[g], ag_s.at[0], ag_r.at[g],
            device_id=y_peers[0], device_id_type=MESH)

    def pair_sum(g, xx):
        mine = part[g, :, :, pl.ds(xx, 1), pl.ds(c, 1)].reshape(8, 16, 128)
        return mine + sib_recv[g, :, :, pl.ds(xx, 1)].reshape(8, 16, 128)

    def send_x(g):
        to_sibling(g).wait_recv()
        for d in (2, 1, 3):
            encode(pair_sum(g, (x + d) % 4), x_send.at[g, d - 1])
            to_x(g, d).start()
        own[g] = pair_sum(g, x)

    def wgrad(g, carry):
        for pair in range(2):
            t = 4 * g + 2 * pair
            both = jnp.concatenate([g_window(t), g_window(t + 1)], axis=1)
            terms = jnp.dot(xt[...], both, preferred_element_type=F32)
            part[g, 2 * pair] = terms[:, :128].reshape(2, 4, 2, 16, 128)
            part[g, 2 * pair + 1] = terms[:, 128:].reshape(2, 4, 2, 16, 128)
        to_sibling(g).start()

        @pl.when(g > 0)
        def _():
            send_x(g - 1)

        return carry

    lax.fori_loop(0, GROUPS, wgrad, 0)
    loads[2].wait()
    send_x(GROUPS - 1)
    halo(xc, xface, xfr, 17, "recv")
    shift_all(xc, xfr, x3)
    acc_f[...] = jnp.zeros_like(acc_f)
    acc_b[...] = jnp.zeros_like(acc_b)

    def convolve(t0, count):
        for t in range(0, count, 2):
            n = min(2, count - t)
            wins = [g_window(t0 + t + i) for i in range(n)]
            kers = [wv[t0 + t + i] for i in range(n)]
            win = jnp.concatenate(wins, axis=1) if n == 2 else wins[0]
            ker = jnp.concatenate(kers, axis=1) if n == 2 else kers[0]
            acc_b[...] += lax.dot_general(win, ker, (((1,), (1,)), ((), ())), preferred_element_type=F32)
        for t in range(count):
            acc_f[...] += jnp.dot(x_window(t0 + t), wv[t0 + t], preferred_element_type=F32)

    def own_group():
        for slot in range(7):
            from_y(slot).wait_recv()
        total = own[y]
        for slot in range(7):
            total = total + decode(y_recv.at[slot], 8)
        total = total.reshape(4, 2, 16, 128)
        for h in range(2):
            encode(total[:, h], z_send.at[h])
        for d in range(1, 8):
            to_z(d).start()
        z_own[...] = jnp.where(zh == 0, total[:, 0], total[:, 1])

    def finish_group():
        for d in range(1, 8):
            to_z(d).wait_recv()
        total = z_own[...]
        for d in range(1, 8):
            total = total + decode(z_recv.at[d - 1], 4)
        kg[y] = total / jnp.sqrt(F32(131072))
        for d in range(1, 8):
            gather(d).start()

    def reduce(g, carry):
        for d in (1, 3, 2):
            to_x(g, d).wait_recv()
        total = own[g]
        for d in (1, 3, 2):
            total = total + decode(x_recv.at[g, d - 1], 8)

        @pl.when(y == g)
        def _():
            own[g] = total

        @pl.when(y != g)
        def _():
            encode(total, y_send.at[g])
            to_y(g).start()

        convolve(4 * g, 3)

        @pl.when(g < GROUPS - 1)
        def _():
            convolve(4 * g + 3, 1)

        @pl.when((g >= 2) & (y == g - 2))
        def _():
            own_group()

        @pl.when((g >= 4) & (y == g - 4))
        def _():
            finish_group()

        return carry

    lax.fori_loop(0, GROUPS, reduce, 0)
    out_v[...] = acc_f[...].astype(BF16).reshape(2, 8, 16, 128)
    back_v[...] = acc_b[...].astype(BF16).reshape(2, 8, 16, 256)
    stores = [
        pltpu.make_async_copy(out_v, out_hbm, out_sem.at[0]),
        pltpu.make_async_copy(back_v, back_hbm, out_sem.at[1]),
    ]
    for store in stores:
        store.start()

    @pl.when((y >= 5) & (y < GROUPS))
    def _():
        own_group()

    @pl.when((y >= 3) & (y < GROUPS))
    def _():
        finish_group()

    halo(gc, gface, gfr, 0, "send")
    halo(xc, xface, xfr, 17, "send")

    def sent(g, carry):
        to_sibling(g).wait_send()
        for d in (1, 2, 3):
            to_x(g, d).wait_send()

        @pl.when(y != g)
        def _():
            to_y(g).wait_send()

        return carry

    lax.fori_loop(0, GROUPS, sent, 0)

    @pl.when(y < GROUPS)
    def _():
        for d in range(1, 8):
            to_z(d).wait_send()
            gather(d).wait_send()

    def arrived(g, carry):
        @pl.when(y != g)
        def _():
            gathered(g).wait_recv()

        return carry

    lax.fori_loop(0, GROUPS, arrived, 0)
    last = pltpu.make_async_copy(kg, kg_hbm, out_sem.at[2])
    last.start()
    for store in stores:
        store.wait()
    last.wait()


def per_device(volumes, weights, out_grads):
    vm = pltpu.VMEM
    dma = pltpu.SemaphoreType.DMA
    any_space = pl.BlockSpec(memory_space=pl.ANY)
    out, back, kg = pl.pallas_call(
        kernel,
        out_shape=(
            jax.ShapeDtypeStruct((2, 8, 16, 128), BF16),
            jax.ShapeDtypeStruct((2, 8, 16, 256), BF16),
            jax.ShapeDtypeStruct((GROUPS, 4, 16, 128), F32),
        ),
        in_specs=[any_space] * 3,
        out_specs=(any_space,) * 3,
        scratch_shapes=[
            vm((27, 256, 128), BF16), vm((4, 10, 16, 256), BF16), vm((4, 10, 16, 128), BF16),
            vm((3, 4, 10, 16, 256), BF16), vm((3, 4, 10, 16, 128), BF16),
            vm((16, 256), BF16), vm((16, 128), BF16), vm((3, 3, 16, 256), BF16), vm((3, 3, 16, 128), BF16),
            vm((256, 256), BF16),
            vm((GROUPS, 4, 2, 4, 2, 16, 128), F32), vm((GROUPS, 4, 2, 4, 16, 128), F32),
            vm((GROUPS, 3, 9, 16, 128), BF16), vm((GROUPS, 3, 9, 16, 128), BF16),
            vm((GROUPS, 8, 16, 128), F32),
            vm((GROUPS, 9, 16, 128), BF16), vm((7, 9, 16, 128), BF16),
            vm((4, 16, 128), F32), vm((2, 5, 16, 128), BF16), vm((7, 5, 16, 128), BF16),
            vm((GROUPS, 4, 16, 128), F32),
            vm((256, 128), F32), vm((256, 256), F32),
            vm((2, 8, 16, 128), BF16), vm((2, 8, 16, 256), BF16),
            dma((3,)), dma((3,)), dma((34,)), dma((34,)), dma((GROUPS,)), dma((GROUPS,)),
            dma((GROUPS, 3)), dma((GROUPS, 3)), dma((GROUPS,)), dma((7,)), dma((7,)), dma((7,)),
            dma((7,)), dma((GROUPS,)),
        ],
        compiler_params=pltpu.CompilerParams(
            collective_id=0, has_side_effects=True, vmem_limit_bytes=60 * 2**20),
        cost_estimate=pl.CostEstimate(flops=1400000000, bytes_accessed=3000000, transcendentals=0),
    )(volumes.reshape(2, 8, 16, 256), weights.reshape(27, 256, 128), out_grads.reshape(2, 8, 16, 128))
    kg = kg.reshape(28, 16, 128)[:27].reshape(3, 3, 3, 16, 128)
    return out[None, None], back[None, None], kg


def solution(mesh):
    block = P("replica", "space", None, None, None, None)
    return jax.shard_map(
        per_device, mesh=mesh, in_specs=(block, P(), block),
        out_specs=(block, block, P(None, None, None, "replica", None)), check_vma=False)
```

time: 527 us -> 72.9 us (0.14)
  the two profiles are of different devices: /device:TPU:2 before, /device:TPU:16 now
where the time goes in v1:
time: 72.9 us; the launch traced here: 72.7 us
  Pallas kernels  67.4 us (92%)
  local copies, waits for them, and re-layouts  4.68 us (6%)
    pallas_call x1, Pallas kernels, per_device(): pl.pallas_call(kernel, out_shape=(jax.ShapeDtypeStruct((2, 8, 16, 128), B...  67.4 us
    unnamed x2, local copies, waits for them, and re-layouts  3.04 us
    slice x1, local copies, waits for them, and re-layouts, per_device(): kg = kg.reshape(28, 16, 128)[:27].reshape(3, 3, 3, 16, 128)  1.64 us

profile of v1, /device:TPU:16, one launch (start us, length us, event | category | flops | bytes accessed | tf_op | source)
XLA Modules:
  0.0 72.7 jit_solution(15563999305517899592)
XLA Ops:
  0.6 67.4 %shard_map.58 = (bf16[2,8,16,128]{3,2,1,0:T(8,128)(2,1)}, bf16[2,8,16,256]{3,2,1,0:T(8,128)(2,1)}, f32[7,4,16,128]{3,2,1,0:T(8,128)}) custom-call(bf16[2,8,16,256]{3,2,1,0:T(8,128)(2,1)} %bitcast.12, bf16[27,256,128]{2,1,0:T(8,128)(2,1)} %bitcast.11, bf16[2,8,16,128]{3,2,1,0:T(8,128)(2,1)} %bitcast.13), custom_call_target="tpu_custom_call" | custom-call | flops 1400000000 | bytes 3000000 | tf_op jit(solution)/shard_map/pallas_call | solution.py:386
  68.0 1.6 %slice.4 = f32[27,16,128]{2,1,0:T(8,128)} slice(f32[28,16,128]{2,1,0:T(8,128)} %bitcast.8), slice={[0:27], [0:16], [0:128]} | slice | bytes 442368 | tf_op jit(solution)/shard_map/slice | solution.py:416
  69.6 1.5 %copy.8 = bf16[1,1,2,8,16,128]{5,4,3,2,1,0:T(8,128)(2,1)} copy(bf16[1,1,2,8,16,128]{5,4,3,2,1,0:T(8,128)(2,1)} %bitcast.10) | data formatting | bytes 131072
  71.1 1.6 %copy.9 = bf16[1,1,2,8,16,256]{5,4,3,2,1,0:T(8,128)(2,1)} copy(bf16[1,1,2,8,16,256]{5,4,3,2,1,0:T(8,128)(2,1)} %bitcast.9) | data formatting | bytes 262144

commit v2 on v1

v2 whole, which is shorter than its diff:
```python
import jax
import jax.numpy as jnp
from jax import lax
from jax.experimental import pallas as pl
from jax.experimental.pallas import tpu as pltpu
from jax.sharding import PartitionSpec as P

MESH = pl.DeviceIdType.MESH
F32 = jnp.float32
BF16 = jnp.bfloat16
GROUPS = 7
FAR_FIRST = (4, 3, 5, 2, 6, 1, 7)
LIFT = 32768.0
PLANE = [(-1, -1), (-1, 1), (1, -1), (1, 1), (-1, 0), (1, 0), (0, -1), (0, 1), (0, 0)]


def encode(u, msg):
    n = u.shape[0]
    top = jnp.max(jnp.max(jnp.abs(u), axis=0), axis=0, keepdims=True)
    top = jnp.maximum(top, 1e-30).astype(BF16)
    v = u * (LIFT / top.astype(F32))
    v2 = v * v
    v4 = v2 * v2
    msg[pl.ds(0, n)] = ((v4 * v2) * (v * jnp.abs(v))).astype(BF16)
    msg[n] = jnp.broadcast_to(top.astype(F32), (16, 128)).astype(BF16)


def decode(msg, n):
    y = msg[pl.ds(0, n)].astype(F32)
    scale = msg[n].astype(F32) * (1.0 / LIFT)
    a = jnp.abs(y)
    t = lax.rsqrt(lax.rsqrt(a))
    u = jnp.where(a == 0.0, 0.0, t * lax.rsqrt(t))
    return jnp.where(y < 0.0, -u, u) * scale


def kernel(
    x_hbm, w_hbm, g_hbm, out_ref, back_ref, kg_ref,
    wv, xc, gc, x3, g3, xface, gface, xfr, gfr, xt,
    part, sib_recv, x_send, x_recv, own, y_send, y_recv, z_send, z_recv, done, acc_f, acc_b,
    in_sem, halo_s, halo_r, sib_s, sib_r, xs_s, xs_r, ys_s, ys_r, zs_s, zs_r, ag_s, ag_r,
):
    s = lax.axis_index("space")
    r = lax.axis_index("replica")
    y, zl = s // 4, s % 4
    zh, x, c = r // 8, (r // 2) % 4, r % 2
    gx, gy, gz = s // 8, (s // 2) % 4, s % 2

    loads = [
        pltpu.make_async_copy(g_hbm, gc.at[pl.ds(1, 2), pl.ds(1, 8)], in_sem.at[0]),
        pltpu.make_async_copy(x_hbm, xc.at[pl.ds(1, 2), pl.ds(1, 8)], in_sem.at[1]),
        pltpu.make_async_copy(w_hbm, wv, in_sem.at[2]),
    ]
    for load in loads:
        load.start()
    for field in (gc, xc):
        none = jnp.zeros((1, 10, 16, field.shape[3]), BF16)
        field[pl.ds(0, 1)] = none
        field[pl.ds(3, 1)] = none
        none = jnp.zeros((2, 1, 16, field.shape[3]), BF16)
        field[pl.ds(1, 2), pl.ds(0, 1)] = none
        field[pl.ds(1, 2), pl.ds(9, 1)] = none
    gfr[...] = jnp.zeros_like(gfr)
    xfr[...] = jnp.zeros_like(xfr)

    def inside(ox, oy):
        return (gx + ox >= 0) & (gx + ox <= 3) & (gy + oy >= 0) & (gy + oy <= 3)

    def at(ox, oy, other):
        return ((gx + ox) * 8 + (gy + oy) * 2 + (1 - gz if other else gz), r)

    z = zh * 4 + zl
    sibling = (s, r + 1 - 2 * c)
    x_peers = [(s, zh * 8 + ((x + d) % 4) * 2 + c) for d in (1, 2, 3)]
    y_peers = {d: (((y + d) % 8) * 4 + zl, r) for d in FAR_FIRST}

    def z_peer(d):
        z_to = (z + d) % 8
        return (y * 4 + z_to % 4, (z_to // 4) * 8 + x * 2 + c)

    z_peers = {d: z_peer(d) for d in FAR_FIRST}

    barrier = pltpu.get_barrier_semaphore()

    def greet(who):
        pl.semaphore_signal(barrier, inc=1, device_id=who, device_id_type=MESH)

    expected = 18
    for ox, oy in PLANE:
        here = inside(ox, oy)
        if (ox, oy) == (0, 0):
            greet(at(0, 0, True))
            expected = expected + 1
            continue

        @pl.when(here)
        def _(ox=ox, oy=oy):
            greet(at(ox, oy, False))
            greet(at(ox, oy, True))

        expected = expected + jnp.where(here, 2, 0)
    for who in x_peers + list(y_peers.values()) + list(z_peers.values()) + [sibling]:
        greet(who)

    def cut(o, size):
        return (pl.ds(0, size), pl.ds(1, size)) if o == 0 else (
            (pl.ds(size - 1, 1), pl.ds(0, 1)) if o == 1 else (pl.ds(0, 1), pl.ds(size + 1, 1)))

    def slab(source, field, k, ox, oy, base):
        (xs, xd), (ys, yd) = cut(ox, 2), cut(oy, 8)
        return pltpu.make_async_remote_copy(
            source.at[xs, ys], field.at[xd, yd], halo_s.at[base + k], halo_r.at[base + k],
            device_id=at(ox, oy, False), device_id_type=MESH)

    def face(source, field, k, ox, oy, base):
        return pltpu.make_async_remote_copy(
            source, field.at[1 - ox, 1 - oy], halo_s.at[base + 8 + k], halo_r.at[base + 8 + k],
            device_id=at(ox, oy, True), device_id_type=MESH)

    def halo(message, source, field, base, do):
        for k, (ox, oy) in enumerate(PLANE):
            here = inside(-ox, -oy) if do == "wait_recv" else inside(ox, oy)
            if (ox, oy) == (0, 0):
                if message is face:
                    getattr(message(source, field, k, ox, oy, base), do)()
                continue

            @pl.when(here)
            def _(k=k, ox=ox, oy=oy):
                getattr(message(source, field, k, ox, oy, base), do)()

    rows = lax.broadcasted_iota(jnp.int32, (16, 256), 0)
    cols = lax.broadcasted_iota(jnp.int32, (16, 256), 1)
    pick = jnp.where(cols == rows * 16 + jnp.where(gz == 0, 15, 0), 1.0, 0.0).astype(BF16)

    def interior(field):
        return field[pl.ds(1, 2), pl.ds(1, 8)].reshape(256, field.shape[3])

    pl.semaphore_wait(barrier, expected)
    halo(slab, g_hbm, gc, 0, "start")
    loads[0].wait()
    gface[...] = jnp.dot(pick, interior(gc), preferred_element_type=F32).astype(BF16)
    halo(face, gface, gfr, 0, "start")
    loads[1].wait()
    xface[...] = jnp.dot(pick, interior(xc), preferred_element_type=F32).astype(BF16)
    xt[...] = interior(xc).T

    def shift_all(field, received, shifted):
        ch = field.shape[3]
        shifted[1] = field[...]
        ri = lax.broadcasted_iota(jnp.int32, (160, 208), 0)
        ci = lax.broadcasted_iota(jnp.int32, (160, 208), 1)
        zi, yi = ri % 16, ri // 16
        for layer in range(4):
            ox = (0, 1, 1, 2)[layer]
            xrow = (8, 0, 8, 0)[layer]
            face_row = jnp.where(yi == 0, 160 + xrow + 7, jnp.where(yi == 9, 192 + xrow, 176 + xrow + yi - 1))
            low_col = jnp.where(zi > 0, ri - 1, jnp.where(gz == 1, face_row, -1))
            high_col = jnp.where(zi < 15, ri + 1, jnp.where(gz == 0, face_row, -1))
            low = jnp.where(ci == low_col, 1.0, 0.0).astype(BF16)
            high = jnp.where(ci == high_col, 1.0, 0.0).astype(BF16)
            cells = jnp.concatenate([field[layer].reshape(160, ch), received[ox].reshape(48, ch)], axis=0)
            shifted[0, layer] = jnp.dot(low, cells, preferred_element_type=F32).astype(BF16).reshape(10, 16, ch)
            shifted[2, layer] = jnp.dot(high, cells, preferred_element_type=F32).astype(BF16).reshape(10, 16, ch)

    def tap_of(t):
        t = jnp.minimum(t, 26)
        return t // 9, (t // 3) % 3, t % 3

    def g_window(t):
        dx, dy, dz = tap_of(t)
        return g3[2 - dz, pl.ds(2 - dx, 2), pl.ds(2 - dy, 8)].reshape(256, 128)

    def x_window(t):
        dx, dy, dz = tap_of(t)
        return x3[dz, pl.ds(dx, 2), pl.ds(dy, 8)].reshape(256, 256)

    halo(slab, g_hbm, gc, 0, "wait_recv")
    halo(face, gface, gfr, 0, "wait_recv")
    shift_all(gc, gfr, g3)
    halo(slab, x_hbm, xc, 17, "start")
    halo(face, xface, xfr, 17, "start")

    def to_sibling(g):
        return pltpu.make_async_remote_copy(
            part.at[g, :, :, :, 1 - c], sib_recv.at[g], sib_s.at[g], sib_r.at[g],
            device_id=sibling, device_id_type=MESH)

    def to_x(g, d):
        return pltpu.make_async_remote_copy(
            x_send.at[g, d - 1], x_recv.at[g, d - 1], xs_s.at[g, d - 1], xs_r.at[g, d - 1],
            device_id=x_peers[d - 1], device_id_type=MESH)

    def to_y(g):
        slot = (g - y + 8) % 8 - 1
        return pltpu.make_async_remote_copy(
            y_send.at[g], y_recv.at[slot], ys_s.at[g], ys_r.at[slot],
            device_id=(g * 4 + zl, r), device_id_type=MESH)

    def from_y(slot):
        return pltpu.make_async_remote_copy(
            y_send.at[0], y_recv.at[slot], ys_s.at[0], ys_r.at[slot],
            device_id=y_peers[1], device_id_type=MESH)

    def to_z(d):
        z_to = (z + d) % 8
        return pltpu.make_async_remote_copy(
            z_send.at[z_to // 4], z_recv.at[z], zs_s.at[d - 1], zs_r.at[z],
            device_id=z_peers[d], device_id_type=MESH)

    def from_z(d):
        z_from = (z + d) % 8
        return pltpu.make_async_remote_copy(
            z_send.at[0], z_recv.at[z_from], zs_s.at[0], zs_r.at[z_from],
            device_id=z_peers[d], device_id_type=MESH)

    def to_all(d):
        return pltpu.make_async_remote_copy(
            done.at[y], done.at[y], ag_s.at[d - 1], ag_r.at[y],
            device_id=y_peers[d], device_id_type=MESH)

    def from_owner(g):
        return pltpu.make_async_remote_copy(
            done.at[g], done.at[g], ag_s.at[0], ag_r.at[g],
            device_id=y_peers[1], device_id_type=MESH)

    def pair_sum(g, xx):
        mine = part[g, :, :, pl.ds(xx, 1), pl.ds(c, 1)].reshape(8, 16, 128)
        return mine + sib_recv[g, :, :, pl.ds(xx, 1)].reshape(8, 16, 128)

    def send_x(g):
        to_sibling(g).wait_recv()
        for d in (2, 1, 3):
            encode(pair_sum(g, (x + d) % 4), x_send.at[g, d - 1])
            to_x(g, d).start()
        own[g] = pair_sum(g, x)

    def wgrad(g, carry):
        for pair in range(2):
            t = 4 * g + 2 * pair
            both = jnp.concatenate([g_window(t), g_window(t + 1)], axis=1)
            terms = jnp.dot(xt[...], both, preferred_element_type=F32)
            part[g, 2 * pair] = terms[:, :128].reshape(2, 4, 2, 16, 128)
            part[g, 2 * pair + 1] = terms[:, 128:].reshape(2, 4, 2, 16, 128)
        to_sibling(g).start()

        @pl.when(g > 0)
        def _():
            send_x(g - 1)

        return carry

    lax.fori_loop(0, GROUPS, wgrad, 0)
    send_x(GROUPS - 1)
    loads[2].wait()
    acc_b[...] = jnp.zeros_like(acc_b)
    acc_f[...] = jnp.zeros_like(acc_f)

    def backward(t0, count):
        for t in range(0, count, 2):
            n = min(2, count - t)
            wins = [g_window(t0 + t + i) for i in range(n)]
            kers = [wv[t0 + t + i] for i in range(n)]
            win = jnp.concatenate(wins, axis=1) if n == 2 else wins[0]
            ker = jnp.concatenate(kers, axis=1) if n == 2 else kers[0]
            acc_b[...] += lax.dot_general(win, ker, (((1,), (1,)), ((), ())), preferred_element_type=F32)

    def reduce(g, carry):
        for d in (1, 3, 2):
            to_x(g, d).wait_recv()
        total = own[g]
        for d in (1, 3, 2):
            total = total + decode(x_recv.at[g, d - 1], 8)

        @pl.when(y == g)
        def _():
            own[g] = total

        @pl.when(y != g)
        def _():
            encode(total, y_send.at[g])
            to_y(g).start()

        backward(4 * g, 3)

        @pl.when(g < GROUPS - 1)
        def _():
            backward(4 * g + 3, 1)

        return carry

    lax.fori_loop(0, GROUPS, reduce, 0)

    halo(slab, x_hbm, xc, 17, "wait_recv")
    halo(face, xface, xfr, 17, "wait_recv")
    shift_all(xc, xfr, x3)

    def forward(k, carry):
        for i in range(3):
            acc_f[...] += jnp.dot(x_window(3 * k + i), wv[3 * k + i], preferred_element_type=F32)
        return carry

    lax.fori_loop(0, 9, forward, 0)

    @pl.when(y < GROUPS)
    def _():
        for slot in range(7):
            from_y(slot).wait_recv()
        total = own[y]
        for slot in range(7):
            total = total + decode(y_recv.at[slot], 8)
        total = total.reshape(4, 2, 16, 128)
        for h in range(2):
            encode(total[:, h], z_send.at[h])
        for d in FAR_FIRST:
            to_z(d).start()
        z_recv[z] = z_send[zh]

    back_ref[...] = acc_b[...].astype(BF16).reshape(2, 8, 16, 256)
    out_ref[...] = acc_f[...].astype(BF16).reshape(2, 8, 16, 128)

    def sent(g, carry):
        to_sibling(g).wait_send()
        for d in (1, 2, 3):
            to_x(g, d).wait_send()

        @pl.when(y != g)
        def _():
            to_y(g).wait_send()

        return carry

    lax.fori_loop(0, GROUPS, sent, 0)
    for source, field, base in ((g_hbm, gc, 0), (x_hbm, xc, 17)):
        halo(slab, source, field, base, "wait_send")
    for source, field, base in ((gface, gfr, 0), (xface, xfr, 17)):
        halo(face, source, field, base, "wait_send")

    @pl.when(y < GROUPS)
    def _():
        for d in FAR_FIRST:
            from_z(d).wait_recv()
        total = decode(z_recv.at[0], 4)
        for k in range(1, 8):
            total = total + decode(z_recv.at[k], 4)
        encode(total / jnp.sqrt(F32(131072)), done.at[y])
        for d in FAR_FIRST:
            to_all(d).start()
        for d in FAR_FIRST:
            to_z(d).wait_send()

    def arrived(g, carry):
        @pl.when(y != g)
        def _():
            from_owner(g).wait_recv()

        kg_ref[g] = decode(done.at[g], 4)
        return carry

    lax.fori_loop(0, GROUPS, arrived, 0)

    @pl.when(y < GROUPS)
    def _():
        for d in FAR_FIRST:
            to_all(d).wait_send()


def per_device(volumes, weights, out_grads):
    vm = pltpu.VMEM
    dma = pltpu.SemaphoreType.DMA
    in_hbm = pl.BlockSpec(memory_space=pltpu.HBM)
    in_vmem = pl.BlockSpec(memory_space=pltpu.VMEM)
    out, back, kg = pl.pallas_call(
        kernel,
        out_shape=(
            jax.ShapeDtypeStruct((2, 8, 16, 128), BF16),
            jax.ShapeDtypeStruct((2, 8, 16, 256), BF16),
            jax.ShapeDtypeStruct((GROUPS, 4, 16, 128), F32),
        ),
        in_specs=[in_hbm] * 3,
        out_specs=(in_vmem,) * 3,
        scratch_shapes=[
            vm((27, 256, 128), BF16), vm((4, 10, 16, 256), BF16), vm((4, 10, 16, 128), BF16),
            vm((3, 4, 10, 16, 256), BF16), vm((3, 4, 10, 16, 128), BF16),
            vm((16, 256), BF16), vm((16, 128), BF16), vm((3, 3, 16, 256), BF16), vm((3, 3, 16, 128), BF16),
            vm((256, 256), BF16),
            vm((GROUPS, 4, 2, 4, 2, 16, 128), F32), vm((GROUPS, 4, 2, 4, 16, 128), F32),
            vm((GROUPS, 3, 9, 16, 128), BF16), vm((GROUPS, 3, 9, 16, 128), BF16),
            vm((GROUPS, 8, 16, 128), F32),
            vm((GROUPS, 9, 16, 128), BF16), vm((7, 9, 16, 128), BF16),
            vm((2, 5, 16, 128), BF16), vm((8, 5, 16, 128), BF16), vm((GROUPS, 5, 16, 128), BF16),
            vm((256, 128), F32), vm((256, 256), F32),
            dma((3,)), dma((34,)), dma((34,)), dma((GROUPS,)), dma((GROUPS,)),
            dma((GROUPS, 3)), dma((GROUPS, 3)), dma((GROUPS,)), dma((7,)), dma((7,)), dma((8,)),
            dma((7,)), dma((GROUPS,)),
        ],
        compiler_params=pltpu.CompilerParams(
            collective_id=0, has_side_effects=True, vmem_limit_bytes=53 * 2**20),
        cost_estimate=pl.CostEstimate(flops=1400000000, bytes_accessed=3000000, transcendentals=0),
    )(volumes.reshape(2, 8, 16, 256), weights.reshape(27, 256, 128), out_grads.reshape(2, 8, 16, 128))
    kg = kg.reshape(28, 16, 128)[:27].reshape(3, 3, 3, 16, 128)
    return out[None, None], back[None, None], kg


def solution(mesh):
    block = P("replica", "space", None, None, None, None)
    return jax.shard_map(
        per_device, mesh=mesh, in_specs=(block, P(), block),
        out_specs=(block, block, P(None, None, None, "replica", None)), check_vma=False)
```

time: 72.9 us -> 60.6 us (0.83)
  the two profiles are of different devices: /device:TPU:16 before, /device:TPU:1 now
where the time goes in v2:
time: 60.6 us; the launch traced here: 60.4 us
  Pallas kernels  56.1 us (93%)
  local copies, waits for them, and re-layouts  3.72 us (6%)
  between operations  0.65 us (1%)
    pallas_call x1, Pallas kernels, per_device(): pl.pallas_call(kernel, out_shape=(jax.ShapeDtypeStruct((2, 8, 16, 128), B...  56.1 us
    unnamed x6, local copies, waits for them, and re-layouts  3.02 us

profile of v2, /device:TPU:1, one launch (start us, length us, event | category | flops | bytes accessed | tf_op | source)
XLA Modules:
  0.0 60.4 jit_solution(12597153999758796138)
XLA Ops:
  0.6 0.0 copy-start
  0.6 0.9 %copy-done = bf16[1,1,2,8,16,256]{5,4,3,2,1,0:T(8,128)(2,1)S(1)} copy-done((bf16[1,1,2,8,16,256]{5,4,3,2,1,0:T(8,128)(2,1)S(1)}, bf16[1,1,2,8,16,256]{5,4,3,2,1,0:T(8,128)(2,1)}, u32[]{:S(2)}) %copy-start) | copy-done | bytes 131096
  1.5 0.0 copy-start.1
  1.5 0.8 %copy-done.1 = bf16[1,1,2,8,16,128]{5,4,3,2,1,0:T(8,128)(2,1)S(1)} copy-done((bf16[1,1,2,8,16,128]{5,4,3,2,1,0:T(8,128)(2,1)S(1)}, bf16[1,1,2,8,16,128]{5,4,3,2,1,0:T(8,128)(2,1)}, u32[]{:S(2)}) %copy-start.1) | copy-done | bytes 65560
  2.4 56.1 %shard_map.58 = (bf16[2,8,16,128]{3,2,1,0:T(8,128)(2,1)S(1)}, bf16[2,8,16,256]{3,2,1,0:T(8,128)(2,1)S(1)}, f32[7,4,16,128]{3,2,1,0:T(8,128)S(1)}) custom-call(bf16[2,8,16,256]{3,2,1,0:T(8,128)(2,1)S(1)} %bitcast.10, bf16[27,256,128]{2,1,0:T(8,128)(2,1)} %bitcast.13, bf16[2,8,16,128]{3,2,1,0:T(8,128)(2,1)S(1)} %bitcast.11), custom_call_target="tpu_custom_call" | custom-call | flops 1400000000 | bytes 3000000 | tf_op jit(solution)/shard_map/pallas_call | solution.py:373
  58.5 0.7 %slice.4 = f32[27,16,128]{2,1,0:T(8,128)} slice(f32[28,16,128]{2,1,0:T(8,128)S(1)} %bitcast.7), slice={[0:27], [0:16], [0:128]} | slice | bytes 442368 | tf_op jit(solution)/shard_map/slice | solution.py:401
  59.2 0.6 %copy.8 = bf16[1,1,2,8,16,128]{5,4,3,2,1,0:T(8,128)(2,1)} copy(bf16[1,1,2,8,16,128]{5,4,3,2,1,0:T(8,128)(2,1)S(1)} %bitcast.9) | data formatting | bytes 131072
  59.8 0.7 %copy.9 = bf16[1,1,2,8,16,256]{5,4,3,2,1,0:T(8,128)(2,1)} copy(bf16[1,1,2,8,16,256]{5,4,3,2,1,0:T(8,128)(2,1)S(1)} %bitcast.8) | data formatting | bytes 262144
Async XLA Ops:
  0.6 0.9 %copy-start = (bf16[1,1,2,8,16,256]{5,4,3,2,1,0:T(8,128)(2,1)S(1)}, bf16[1,1,2,8,16,256]{5,4,3,2,1,0:T(8,128)(2,1)}, u32[]{:S(2)}) copy-start(bf16[1,1,2,8,16,256]{5,4,3,2,1,0:T(8,128)(2,1)} %param.3) | copy-start | bytes 393220
  1.5 0.8 %copy-start.1 = (bf16[1,1,2,8,16,128]{5,4,3,2,1,0:T(8,128)(2,1)S(1)}, bf16[1,1,2,8,16,128]{5,4,3,2,1,0:T(8,128)(2,1)}, u32[]{:S(2)}) copy-start(bf16[1,1,2,8,16,128]{5,4,3,2,1,0:T(8,128)(2,1)} %param.5) | copy-start | bytes 196612

commit v3 on v2

--- a/solution.py
+++ b/solution.py
@@ -36,9 +36,10 @@
 
 def kernel(
     x_hbm, w_hbm, g_hbm, out_ref, back_ref, kg_ref,
-    wv, xc, gc, x3, g3, xface, gface, xfr, gfr, xt,
-    part, sib_recv, x_send, x_recv, own, y_send, y_recv, z_send, z_recv, done, acc_f, acc_b,
-    in_sem, halo_s, halo_r, sib_s, sib_r, xs_s, xs_r, ys_s, ys_r, zs_s, zs_r, ag_s, ag_r,
+    wv, xc, gc, gc2, x3, g3, g32, xface, gface, xfr, gfr, gfr2, xt, xt2,
+    part_a, part_b, x_send, x_recv, own_a, y_send, y_recv, b_send, b_recv, bx_send, bx_recv,
+    z_send, z_recv, done, acc_f, acc_b,
+    in_sem, halo_s, halo_r, sib_s, sib_r, xs_s, xs_r, ys_s, ys_r, bs_s, bs_r, bx_s, bx_r, zs_s, zs_r, ag_s, ag_r,
 ):
     s = lax.axis_index("space")
     r = lax.axis_index("replica")
@@ -129,6 +130,11 @@
             def _(k=k, ox=ox, oy=oy):
                 getattr(message(source, field, k, ox, oy, base), do)()
 
+    def share(k):
+        source, target = ((xt.at[:, 1 - c], xt2), (gc, gc2), (gfr, gfr2))[k]
+        return pltpu.make_async_remote_copy(
+            source, target, sib_s.at[k], sib_r.at[k], device_id=sibling, device_id_type=MESH)
+
     rows = lax.broadcasted_iota(jnp.int32, (16, 256), 0)
     cols = lax.broadcasted_iota(jnp.int32, (16, 256), 1)
     pick = jnp.where(cols == rows * 16 + jnp.where(gz == 0, 15, 0), 1.0, 0.0).astype(BF16)
@@ -143,7 +149,8 @@
     halo(face, gface, gfr, 0, "start")
     loads[1].wait()
     xface[...] = jnp.dot(pick, interior(xc), preferred_element_type=F32).astype(BF16)
-    xt[...] = interior(xc).T
+    xt[...] = interior(xc).T.reshape(8, 2, 16, 256)
+    share(0).start()
 
     def shift_all(field, received, shifted):
         ch = field.shape[3]
@@ -167,9 +174,9 @@
         t = jnp.minimum(t, 26)
         return t // 9, (t // 3) % 3, t % 3
 
-    def g_window(t):
+    def g_window(t, field):
         dx, dy, dz = tap_of(t)
-        return g3[2 - dz, pl.ds(2 - dx, 2), pl.ds(2 - dy, 8)].reshape(256, 128)
+        return field[2 - dz, pl.ds(2 - dx, 2), pl.ds(2 - dy, 8)].reshape(256, 128)
 
     def x_window(t):
         dx, dy, dz = tap_of(t)
@@ -177,20 +184,30 @@
 
     halo(slab, g_hbm, gc, 0, "wait_recv")
     halo(face, gface, gfr, 0, "wait_recv")
+    share(1).start()
+    share(2).start()
     shift_all(gc, gfr, g3)
     halo(slab, x_hbm, xc, 17, "start")
     halo(face, xface, xfr, 17, "start")
-
-    def to_sibling(g):
-        return pltpu.make_async_remote_copy(
-            part.at[g, :, :, :, 1 - c], sib_recv.at[g], sib_s.at[g], sib_r.at[g],
-            device_id=sibling, device_id_type=MESH)
+    for k in (1, 2, 0):
+        share(k).wait_recv()
+    shift_all(gc2, gfr2, g32)
 
     def to_x(g, d):
         return pltpu.make_async_remote_copy(
             x_send.at[g, d - 1], x_recv.at[g, d - 1], xs_s.at[g, d - 1], xs_r.at[g, d - 1],
             device_id=x_peers[d - 1], device_id_type=MESH)
 
+    def to_b(d):
+        return pltpu.make_async_remote_copy(
+            b_send.at[d - 1], b_recv.at[d - 1], bs_s.at[d - 1], bs_r.at[d - 1],
+            device_id=(((y + d) % 8) * 4 + zl, r), device_id_type=MESH)
+
+    def to_bx(d):
+        return pltpu.make_async_remote_copy(
+            bx_send.at[d - 1], bx_recv.at[d - 1], bx_s.at[d - 1], bx_r.at[d - 1],
+            device_id=x_peers[d - 1], device_id_type=MESH)
+
     def to_y(g):
         slot = (g - y + 8) % 8 - 1
         return pltpu.make_async_remote_copy(
@@ -224,34 +241,37 @@
             done.at[g], done.at[g], ag_s.at[0], ag_r.at[g],
             device_id=y_peers[1], device_id_type=MESH)
 
-    def pair_sum(g, xx):
-        mine = part[g, :, :, pl.ds(xx, 1), pl.ds(c, 1)].reshape(8, 16, 128)
-        return mine + sib_recv[g, :, :, pl.ds(xx, 1)].reshape(8, 16, 128)
-
-    def send_x(g):
-        to_sibling(g).wait_recv()
-        for d in (2, 1, 3):
-            encode(pair_sum(g, (x + d) % 4), x_send.at[g, d - 1])
-            to_x(g, d).start()
-        own[g] = pair_sum(g, x)
-
-    def wgrad(g, carry):
-        for pair in range(2):
-            t = 4 * g + 2 * pair
-            both = jnp.concatenate([g_window(t), g_window(t + 1)], axis=1)
-            terms = jnp.dot(xt[...], both, preferred_element_type=F32)
-            part[g, 2 * pair] = terms[:, :128].reshape(2, 4, 2, 16, 128)
-            part[g, 2 * pair + 1] = terms[:, 128:].reshape(2, 4, 2, 16, 128)
-        to_sibling(g).start()
-
-        @pl.when(g > 0)
-        def _():
-            send_x(g - 1)
+    def products(t):
+        terms = jnp.zeros((128, 256), F32)
+        for field, chans in ((g3, xt[:, c]), (g32, xt2[...])):
+            both = jnp.concatenate([g_window(t, field), g_window(t + 1, field)], axis=1)
+            terms = terms + jnp.dot(chans.reshape(128, 256), both, preferred_element_type=F32)
+        return [terms[:, 128 * i : 128 * i + 128].reshape(2, 4, 16, 128) for i in range(2)]
+
+    def step(i):
+        dy = 4 + ((i + 1) // 2) * (1 - 2 * (i % 2))
+        return dy, (y + dy) % 8
+
+    def wgrad(i, carry):
+        dy, q = step(i)
+
+        @pl.when(q < GROUPS)
+        def _():
+            part_a[q, 2], part_b[...] = products(4 * q + 2)
+
+            @pl.when(dy != 0)
+            def _():
+                encode(part_b[...].reshape(8, 16, 128), b_send.at[dy - 1])
+                to_b(dy).start()
+
+            part_a[q, 0], part_a[q, 1] = products(4 * q)
+            for d in (2, 1, 3):
+                encode(part_a[q, :, :, (x + d) % 4].reshape(6, 16, 128), x_send.at[q, d - 1])
+                to_x(q, d).start()
 
         return carry
 
-    lax.fori_loop(0, GROUPS, wgrad, 0)
-    send_x(GROUPS - 1)
+    lax.fori_loop(0, 8, wgrad, 0)
     loads[2].wait()
     acc_b[...] = jnp.zeros_like(acc_b)
     acc_f[...] = jnp.zeros_like(acc_f)
@@ -259,37 +279,55 @@
     def backward(t0, count):
         for t in range(0, count, 2):
             n = min(2, count - t)
-            wins = [g_window(t0 + t + i) for i in range(n)]
+            wins = [g_window(t0 + t + i, g3) for i in range(n)]
             kers = [wv[t0 + t + i] for i in range(n)]
             win = jnp.concatenate(wins, axis=1) if n == 2 else wins[0]
             ker = jnp.concatenate(kers, axis=1) if n == 2 else kers[0]
             acc_b[...] += lax.dot_general(win, ker, (((1,), (1,)), ((), ())), preferred_element_type=F32)
 
-    def reduce(g, carry):
-        for d in (1, 3, 2):
-            to_x(g, d).wait_recv()
-        total = own[g]
-        for d in (1, 3, 2):
-            total = total + decode(x_recv.at[g, d - 1], 8)
-
-        @pl.when(y == g)
-        def _():
-            own[g] = total
-
-        @pl.when(y != g)
-        def _():
-            encode(total, y_send.at[g])
-            to_y(g).start()
-
-        backward(4 * g, 3)
-
-        @pl.when(g < GROUPS - 1)
-        def _():
-            backward(4 * g + 3, 1)
+    def reduce(i, carry):
+        dy, q = step(i)
+
+        @pl.when(q < GROUPS)
+        def _():
+            for d in (1, 3, 2):
+                to_x(q, d).wait_recv()
+            total = part_a[q, :, :, x].reshape(6, 16, 128)
+            for d in (1, 3, 2):
+                total = total + decode(x_recv.at[q, d - 1], 6)
+
+            @pl.when(dy == 0)
+            def _():
+                own_a[...] = total
+
+            @pl.when(dy != 0)
+            def _():
+                encode(total, y_send.at[q])
+                to_y(q).start()
+
+        @pl.when(i < GROUPS)
+        def _():
+            backward(4 * i, 3)
+
+        @pl.when(i < GROUPS - 1)
+        def _():
+            backward(4 * i + 3, 1)
 
         return carry
 
-    lax.fori_loop(0, GROUPS, reduce, 0)
+    lax.fori_loop(0, 8, reduce, 0)
+
+    @pl.when(y < GROUPS)
+    def _():
+        for d in range(1, 8):
+            to_b(d).wait_recv()
+        total = part_b[...].reshape(8, 16, 128)
+        for d in range(1, 8):
+            total = total + decode(b_recv.at[d - 1], 8)
+        part_b[...] = total.reshape(2, 4, 16, 128)
+        for d in (2, 1, 3):
+            encode(part_b[:, (x + d) % 4], bx_send.at[d - 1])
+            to_bx(d).start()
 
     halo(slab, x_hbm, xc, 17, "wait_recv")
     halo(face, xface, xfr, 17, "wait_recv")
@@ -306,10 +344,14 @@
     def _():
         for slot in range(7):
             from_y(slot).wait_recv()
-        total = own[y]
+        first = own_a[...]
         for slot in range(7):
-            total = total + decode(y_recv.at[slot], 8)
-        total = total.reshape(4, 2, 16, 128)
+            first = first + decode(y_recv.at[slot], 6)
+        second = part_b[:, x]
+        for d in (1, 2, 3):
+            to_bx(d).wait_recv()
+            second = second + decode(bx_recv.at[d - 1], 2)
+        total = jnp.concatenate([first, second], axis=0).reshape(4, 2, 16, 128)
         for h in range(2):
             encode(total[:, h], z_send.at[h])
         for d in FAR_FIRST:
@@ -320,7 +362,6 @@
     out_ref[...] = acc_f[...].astype(BF16).reshape(2, 8, 16, 128)
 
     def sent(g, carry):
-        to_sibling(g).wait_send()
         for d in (1, 2, 3):
             to_x(g, d).wait_send()
 
@@ -331,6 +372,12 @@
         return carry
 
     lax.fori_loop(0, GROUPS, sent, 0)
+    for k in range(3):
+        share(k).wait_send()
+    for d in range(1, 8):
+        @pl.when((y + d) % 8 < GROUPS)
+        def _(d=d):
+            to_b(d).wait_send()
     for source, field, base in ((g_hbm, gc, 0), (x_hbm, xc, 17)):
         halo(slab, source, field, base, "wait_send")
     for source, field, base in ((gface, gfr, 0), (xface, xfr, 17)):
@@ -348,6 +395,8 @@
             to_all(d).start()
         for d in FAR_FIRST:
             to_z(d).wait_send()
+        for d in (1, 2, 3):
+            to_bx(d).wait_send()
 
     def arrived(g, carry):
         @pl.when(y != g)
@@ -380,18 +429,20 @@
         in_specs=[in_hbm] * 3,
         out_specs=(in_vmem,) * 3,
         scratch_shapes=[
-            vm((27, 256, 128), BF16), vm((4, 10, 16, 256), BF16), vm((4, 10, 16, 128), BF16),
-            vm((3, 4, 10, 16, 256), BF16), vm((3, 4, 10, 16, 128), BF16),
+            vm((27, 256, 128), BF16), vm((4, 10, 16, 256), BF16), vm((4, 10, 16, 128), BF16), vm((4, 10, 16, 128), BF16),
+            vm((3, 4, 10, 16, 256), BF16), vm((3, 4, 10, 16, 128), BF16), vm((3, 4, 10, 16, 128), BF16),
             vm((16, 256), BF16), vm((16, 128), BF16), vm((3, 3, 16, 256), BF16), vm((3, 3, 16, 128), BF16),
-            vm((256, 256), BF16),
-            vm((GROUPS, 4, 2, 4, 2, 16, 128), F32), vm((GROUPS, 4, 2, 4, 16, 128), F32),
-            vm((GROUPS, 3, 9, 16, 128), BF16), vm((GROUPS, 3, 9, 16, 128), BF16),
-            vm((GROUPS, 8, 16, 128), F32),
-            vm((GROUPS, 9, 16, 128), BF16), vm((7, 9, 16, 128), BF16),
+            vm((3, 3, 16, 128), BF16), vm((8, 2, 16, 256), BF16), vm((8, 16, 256), BF16),
+            vm((GROUPS, 3, 2, 4, 16, 128), F32), vm((2, 4, 16, 128), F32),
+            vm((GROUPS, 3, 7, 16, 128), BF16), vm((GROUPS, 3, 7, 16, 128), BF16), vm((6, 16, 128), F32),
+            vm((GROUPS, 7, 16, 128), BF16), vm((7, 7, 16, 128), BF16),
+            vm((7, 9, 16, 128), BF16), vm((7, 9, 16, 128), BF16),
+            vm((3, 3, 16, 128), BF16), vm((3, 3, 16, 128), BF16),
             vm((2, 5, 16, 128), BF16), vm((8, 5, 16, 128), BF16), vm((GROUPS, 5, 16, 128), BF16),
             vm((256, 128), F32), vm((256, 256), F32),
-            dma((3,)), dma((34,)), dma((34,)), dma((GROUPS,)), dma((GROUPS,)),
-            dma((GROUPS, 3)), dma((GROUPS, 3)), dma((GROUPS,)), dma((7,)), dma((7,)), dma((8,)),
+            dma((3,)), dma((34,)), dma((34,)), dma((3,)), dma((3,)),
+            dma((GROUPS, 3)), dma((GROUPS, 3)), dma((GROUPS,)), dma((7,)),
+            dma((7,)), dma((7,)), dma((3,)), dma((3,)), dma((7,)), dma((8,)),
             dma((7,)), dma((GROUPS,)),
         ],
         compiler_params=pltpu.CompilerParams(

time: 60.6 us -> 56 us (0.924)
  the two profiles are of different devices: /device:TPU:1 before, /device:TPU:8 now
where the time goes in v3:
time: 56 us; the launch traced here: 55.8 us
  Pallas kernels  51.4 us (92%)
  local copies, waits for them, and re-layouts  3.72 us (7%)
  between operations  0.65 us (1%)
    pallas_call x1, Pallas kernels, per_device(): pl.pallas_call(kernel, out_shape=(jax.ShapeDtypeStruct((2, 8, 16, 128), B...  51.4 us
    unnamed x6, local copies, waits for them, and re-layouts  3.02 us

profile of v3, /device:TPU:8, one launch (start us, length us, event | category | flops | bytes accessed | tf_op | source)
XLA Modules:
  0.0 55.8 jit_solution(13494118149504640026)
XLA Ops:
  0.6 0.0 copy-start
  0.6 0.9 %copy-done = bf16[1,1,2,8,16,256]{5,4,3,2,1,0:T(8,128)(2,1)S(1)} copy-done((bf16[1,1,2,8,16,256]{5,4,3,2,1,0:T(8,128)(2,1)S(1)}, bf16[1,1,2,8,16,256]{5,4,3,2,1,0:T(8,128)(2,1)}, u32[]{:S(2)}) %copy-start) | copy-done | bytes 131096
  1.5 0.0 copy-start.1
  1.5 0.8 %copy-done.1 = bf16[1,1,2,8,16,128]{5,4,3,2,1,0:T(8,128)(2,1)S(1)} copy-done((bf16[1,1,2,8,16,128]{5,4,3,2,1,0:T(8,128)(2,1)S(1)}, bf16[1,1,2,8,16,128]{5,4,3,2,1,0:T(8,128)(2,1)}, u32[]{:S(2)}) %copy-start.1) | copy-done | bytes 65560
  2.4 51.4 %shard_map.58 = (bf16[2,8,16,128]{3,2,1,0:T(8,128)(2,1)S(1)}, bf16[2,8,16,256]{3,2,1,0:T(8,128)(2,1)S(1)}, f32[7,4,16,128]{3,2,1,0:T(8,128)S(1)}) custom-call(bf16[2,8,16,256]{3,2,1,0:T(8,128)(2,1)S(1)} %bitcast.10, bf16[27,256,128]{2,1,0:T(8,128)(2,1)} %bitcast.13, bf16[2,8,16,128]{3,2,1,0:T(8,128)(2,1)S(1)} %bitcast.11), custom_call_target="tpu_custom_call" | custom-call | flops 1400000000 | bytes 3000000 | tf_op jit(solution)/shard_map/pallas_call | solution.py:422
  53.8 0.7 %slice.4 = f32[27,16,128]{2,1,0:T(8,128)} slice(f32[28,16,128]{2,1,0:T(8,128)S(1)} %bitcast.7), slice={[0:27], [0:16], [0:128]} | slice | bytes 442368 | tf_op jit(solution)/shard_map/slice | solution.py:452
  54.5 0.6 %copy.8 = bf16[1,1,2,8,16,128]{5,4,3,2,1,0:T(8,128)(2,1)} copy(bf16[1,1,2,8,16,128]{5,4,3,2,1,0:T(8,128)(2,1)S(1)} %bitcast.9) | data formatting | bytes 131072
  55.1 0.7 %copy.9 = bf16[1,1,2,8,16,256]{5,4,3,2,1,0:T(8,128)(2,1)} copy(bf16[1,1,2,8,16,256]{5,4,3,2,1,0:T(8,128)(2,1)S(1)} %bitcast.8) | data formatting | bytes 262144
Async XLA Ops:
  0.6 0.9 %copy-start = (bf16[1,1,2,8,16,256]{5,4,3,2,1,0:T(8,128)(2,1)S(1)}, bf16[1,1,2,8,16,256]{5,4,3,2,1,0:T(8,128)(2,1)}, u32[]{:S(2)}) copy-start(bf16[1,1,2,8,16,256]{5,4,3,2,1,0:T(8,128)(2,1)} %param.3) | copy-start | bytes 393220
  1.5 0.8 %copy-start.1 = (bf16[1,1,2,8,16,128]{5,4,3,2,1,0:T(8,128)(2,1)S(1)}, bf16[1,1,2,8,16,128]{5,4,3,2,1,0:T(8,128)(2,1)}, u32[]{:S(2)}) copy-start(bf16[1,1,2,8,16,128]{5,4,3,2,1,0:T(8,128)(2,1)} %param.5) | copy-start | bytes 196612

commit v4 on v3

--- a/solution.py
+++ b/solution.py
@@ -319,10 +319,9 @@
 
     @pl.when(y < GROUPS)
     def _():
-        for d in range(1, 8):
+        total = part_b[...].reshape(8, 16, 128)
+        for d in FAR_FIRST:
             to_b(d).wait_recv()
-        total = part_b[...].reshape(8, 16, 128)
-        for d in range(1, 8):
             total = total + decode(b_recv.at[d - 1], 8)
         part_b[...] = total.reshape(2, 4, 16, 128)
         for d in (2, 1, 3):
@@ -342,11 +341,10 @@
 
     @pl.when(y < GROUPS)
     def _():
-        for slot in range(7):
-            from_y(slot).wait_recv()
         first = own_a[...]
-        for slot in range(7):
-            first = first + decode(y_recv.at[slot], 6)
+        for d in FAR_FIRST:
+            from_y(d - 1).wait_recv()
+            first = first + decode(y_recv.at[d - 1], 6)
         second = part_b[:, x]
         for d in (1, 2, 3):
             to_bx(d).wait_recv()
@@ -446,9 +444,10 @@
             dma((7,)), dma((GROUPS,)),
         ],
         compiler_params=pltpu.CompilerParams(
-            collective_id=0, has_side_effects=True, vmem_limit_bytes=53 * 2**20),
+            collective_id=0, has_side_effects=True, vmem_limit_bytes=40 * 2**20),
         cost_estimate=pl.CostEstimate(flops=1400000000, bytes_accessed=3000000, transcendentals=0),
-    )(volumes.reshape(2, 8, 16, 256), weights.reshape(27, 256, 128), out_grads.reshape(2, 8, 16, 128))
+    )(*(pltpu.with_memory_space_constraint(array, pltpu.HBM) for array in (
+        volumes.reshape(2, 8, 16, 256), weights.reshape(27, 256, 128), out_grads.reshape(2, 8, 16, 128))))
     kg = kg.reshape(28, 16, 128)[:27].reshape(3, 3, 3, 16, 128)
     return out[None, None], back[None, None], kg
 

time: 56 us -> 54.1 us (0.966)
  local copies, waits for them, and re-layouts: 3.72 us -> 1.98 us
    unnamed x6 -> x2, local copies, waits for them, and re-layouts: 3.02 us -> 1.28 us
where the time goes in v4:
time: 54.1 us; the launch traced here: 54 us
  Pallas kernels  51.3 us (95%)
  local copies, waits for them, and re-layouts  1.98 us (4%)
  between operations  0.64 us (1%)
    pallas_call x1, Pallas kernels, per_device(): pl.pallas_call(kernel, out_shape=(jax.ShapeDtypeStruct((2, 8, 16, 128), B...  51.3 us
    unnamed x2, local copies, waits for them, and re-layouts  1.28 us

profile of v4, /device:TPU:8, one launch (start us, length us, event | category | flops | bytes accessed | tf_op | source)
XLA Modules:
  0.0 54.0 jit_solution(2322113012857542556)
XLA Ops:
  0.6 51.3 %shard_map.58 = (bf16[2,8,16,128]{3,2,1,0:T(8,128)(2,1)S(1)}, bf16[2,8,16,256]{3,2,1,0:T(8,128)(2,1)S(1)}, f32[7,4,16,128]{3,2,1,0:T(8,128)S(1)}) custom-call(bf16[2,8,16,256]{3,2,1,0:T(8,128)(2,1)} %bitcast.12, bf16[27,256,128]{2,1,0:T(8,128)(2,1)} %bitcast.11, bf16[2,8,16,128]{3,2,1,0:T(8,128)(2,1)} %bitcast.13), custom_call_target="tpu_custom_call" | custom-call | flops 1400000000 | bytes 3000000 | tf_op jit(solution)/shard_map/pallas_call | solution.py:420
  52.0 0.7 %slice.4 = f32[27,16,128]{2,1,0:T(8,128)} slice(f32[28,16,128]{2,1,0:T(8,128)S(1)} %bitcast.7), slice={[0:27], [0:16], [0:128]} | slice | bytes 442368 | tf_op jit(solution)/shard_map/slice | solution.py:451
  52.7 0.6 %copy.8 = bf16[1,1,2,8,16,128]{5,4,3,2,1,0:T(8,128)(2,1)} copy(bf16[1,1,2,8,16,128]{5,4,3,2,1,0:T(8,128)(2,1)S(1)} %bitcast.9) | data formatting | bytes 131072
  53.3 0.7 %copy.9 = bf16[1,1,2,8,16,256]{5,4,3,2,1,0:T(8,128)(2,1)} copy(bf16[1,1,2,8,16,256]{5,4,3,2,1,0:T(8,128)(2,1)S(1)} %bitcast.8) | data formatting | bytes 262144

commit v5 on v4

--- a/solution.py
+++ b/solution.py
@@ -332,13 +332,6 @@
     halo(face, xface, xfr, 17, "wait_recv")
     shift_all(xc, xfr, x3)
 
-    def forward(k, carry):
-        for i in range(3):
-            acc_f[...] += jnp.dot(x_window(3 * k + i), wv[3 * k + i], preferred_element_type=F32)
-        return carry
-
-    lax.fori_loop(0, 9, forward, 0)
-
     @pl.when(y < GROUPS)
     def _():
         first = own_a[...]
@@ -356,8 +349,30 @@
             to_z(d).start()
         z_recv[z] = z_send[zh]
 
+    def forward(k, carry):
+        for i in range(3):
+            acc_f[...] += jnp.dot(x_window(3 * k + i), wv[3 * k + i], preferred_element_type=F32)
+        return carry
+
+    lax.fori_loop(0, 9, forward, 0)
+
     back_ref[...] = acc_b[...].astype(BF16).reshape(2, 8, 16, 256)
     out_ref[...] = acc_f[...].astype(BF16).reshape(2, 8, 16, 128)
+
+    @pl.when(y < GROUPS)
+    def _():
+        for d in FAR_FIRST:
+            from_z(d).wait_recv()
+        total = decode(z_recv.at[0], 4)
+        for k in range(1, 8):
+            total = total + decode(z_recv.at[k], 4)
+        encode(total / jnp.sqrt(F32(131072)), done.at[y])
+        for d in FAR_FIRST:
+            to_all(d).start()
+        for d in FAR_FIRST:
+            to_z(d).wait_send()
+        for d in (1, 2, 3):
+            to_bx(d).wait_send()
 
     def sent(g, carry):
         for d in (1, 2, 3):
@@ -380,21 +395,6 @@
         halo(slab, source, field, base, "wait_send")
     for source, field, base in ((gface, gfr, 0), (xface, xfr, 17)):
         halo(face, source, field, base, "wait_send")
-
-    @pl.when(y < GROUPS)
-    def _():
-        for d in FAR_FIRST:
-            from_z(d).wait_recv()
-        total = decode(z_recv.at[0], 4)
-        for k in range(1, 8):
-            total = total + decode(z_recv.at[k], 4)
-        encode(total / jnp.sqrt(F32(131072)), done.at[y])
-        for d in FAR_FIRST:
-            to_all(d).start()
-        for d in FAR_FIRST:
-            to_z(d).wait_send()
-        for d in (1, 2, 3):
-            to_bx(d).wait_send()
 
     def arrived(g, carry):
         @pl.when(y != g)

time: 54.1 us -> 54.1 us (level)
  no operation moved by 1% of the time
where the time goes in v5:
time: 54.1 us; the launch traced here: 54 us
  Pallas kernels  51.3 us (95%)
  local copies, waits for them, and re-layouts  1.98 us (4%)
  between operations  0.64 us (1%)
    pallas_call x1, Pallas kernels, per_device(): pl.pallas_call(kernel, out_shape=(jax.ShapeDtypeStruct((2, 8, 16, 128), B...  51.3 us
    unnamed x2, local copies, waits for them, and re-layouts  1.28 us

profile of v5, /device:TPU:8, one launch (start us, length us, event | category | flops | bytes accessed | tf_op | source)
XLA Modules:
  0.0 54.0 jit_solution(6845778714371318102)
XLA Ops:
  0.6 51.3 %shard_map.58 = (bf16[2,8,16,128]{3,2,1,0:T(8,128)(2,1)S(1)}, bf16[2,8,16,256]{3,2,1,0:T(8,128)(2,1)S(1)}, f32[7,4,16,128]{3,2,1,0:T(8,128)S(1)}) custom-call(bf16[2,8,16,256]{3,2,1,0:T(8,128)(2,1)} %bitcast.12, bf16[27,256,128]{2,1,0:T(8,128)(2,1)} %bitcast.11, bf16[2,8,16,128]{3,2,1,0:T(8,128)(2,1)} %bitcast.13), custom_call_target="tpu_custom_call" | custom-call | flops 1400000000 | bytes 3000000 | tf_op jit(solution)/shard_map/pallas_call | solution.py:420
  52.0 0.7 %slice.4 = f32[27,16,128]{2,1,0:T(8,128)} slice(f32[28,16,128]{2,1,0:T(8,128)S(1)} %bitcast.7), slice={[0:27], [0:16], [0:128]} | slice | bytes 442368 | tf_op jit(solution)/shard_map/slice | solution.py:451
  52.7 0.6 %copy.8 = bf16[1,1,2,8,16,128]{5,4,3,2,1,0:T(8,128)(2,1)} copy(bf16[1,1,2,8,16,128]{5,4,3,2,1,0:T(8,128)(2,1)S(1)} %bitcast.9) | data formatting | bytes 131072
  53.3 0.7 %copy.9 = bf16[1,1,2,8,16,256]{5,4,3,2,1,0:T(8,128)(2,1)} copy(bf16[1,1,2,8,16,256]{5,4,3,2,1,0:T(8,128)(2,1)S(1)} %bitcast.8) | data formatting | bytes 262144

commit v6 on v5

--- a/solution.py
+++ b/solution.py
@@ -37,9 +37,9 @@
 def kernel(
     x_hbm, w_hbm, g_hbm, out_ref, back_ref, kg_ref,
     wv, xc, gc, gc2, x3, g3, g32, xface, gface, xfr, gfr, gfr2, xt, xt2,
-    part_a, part_b, x_send, x_recv, own_a, y_send, y_recv, b_send, b_recv, bx_send, bx_recv,
+    part_a, x_send, x_recv, own_a, y_send, y_recv,
     z_send, z_recv, done, acc_f, acc_b,
-    in_sem, halo_s, halo_r, sib_s, sib_r, xs_s, xs_r, ys_s, ys_r, bs_s, bs_r, bx_s, bx_r, zs_s, zs_r, ag_s, ag_r,
+    in_sem, halo_s, halo_r, sib_s, sib_r, xs_s, xs_r, ys_s, ys_r, zs_s, zs_r, ag_s, ag_r,
 ):
     s = lax.axis_index("space")
     r = lax.axis_index("replica")
@@ -198,16 +198,6 @@
             x_send.at[g, d - 1], x_recv.at[g, d - 1], xs_s.at[g, d - 1], xs_r.at[g, d - 1],
             device_id=x_peers[d - 1], device_id_type=MESH)
 
-    def to_b(d):
-        return pltpu.make_async_remote_copy(
-            b_send.at[d - 1], b_recv.at[d - 1], bs_s.at[d - 1], bs_r.at[d - 1],
-            device_id=(((y + d) % 8) * 4 + zl, r), device_id_type=MESH)
-
-    def to_bx(d):
-        return pltpu.make_async_remote_copy(
-            bx_send.at[d - 1], bx_recv.at[d - 1], bx_s.at[d - 1], bx_r.at[d - 1],
-            device_id=x_peers[d - 1], device_id_type=MESH)
-
     def to_y(g):
         slot = (g - y + 8) % 8 - 1
         return pltpu.make_async_remote_copy(
@@ -257,16 +247,10 @@
 
         @pl.when(q < GROUPS)
         def _():
-            part_a[q, 2], part_b[...] = products(4 * q + 2)
-
-            @pl.when(dy != 0)
-            def _():
-                encode(part_b[...].reshape(8, 16, 128), b_send.at[dy - 1])
-                to_b(dy).start()
-
-            part_a[q, 0], part_a[q, 1] = products(4 * q)
+            for k in (0, 2):
+                part_a[q, k], part_a[q, k + 1] = products(4 * q + k)
             for d in (2, 1, 3):
-                encode(part_a[q, :, :, (x + d) % 4].reshape(6, 16, 128), x_send.at[q, d - 1])
+                encode(part_a[q, :, :, (x + d) % 4].reshape(8, 16, 128), x_send.at[q, d - 1])
                 to_x(q, d).start()
 
         return carry
@@ -292,9 +276,9 @@
         def _():
             for d in (1, 3, 2):
                 to_x(q, d).wait_recv()
-            total = part_a[q, :, :, x].reshape(6, 16, 128)
+            total = part_a[q, :, :, x].reshape(8, 16, 128)
             for d in (1, 3, 2):
-                total = total + decode(x_recv.at[q, d - 1], 6)
+                total = total + decode(x_recv.at[q, d - 1], 8)
 
             @pl.when(dy == 0)
             def _():
@@ -317,17 +301,6 @@
 
     lax.fori_loop(0, 8, reduce, 0)
 
-    @pl.when(y < GROUPS)
-    def _():
-        total = part_b[...].reshape(8, 16, 128)
-        for d in FAR_FIRST:
-            to_b(d).wait_recv()
-            total = total + decode(b_recv.at[d - 1], 8)
-        part_b[...] = total.reshape(2, 4, 16, 128)
-        for d in (2, 1, 3):
-            encode(part_b[:, (x + d) % 4], bx_send.at[d - 1])
-            to_bx(d).start()
-
     halo(slab, x_hbm, xc, 17, "wait_recv")
     halo(face, xface, xfr, 17, "wait_recv")
     shift_all(xc, xfr, x3)
@@ -337,12 +310,8 @@
         first = own_a[...]
         for d in FAR_FIRST:
             from_y(d - 1).wait_recv()
-            first = first + decode(y_recv.at[d - 1], 6)
-        second = part_b[:, x]
-        for d in (1, 2, 3):
-            to_bx(d).wait_recv()
-            second = second + decode(bx_recv.at[d - 1], 2)
-        total = jnp.concatenate([first, second], axis=0).reshape(4, 2, 16, 128)
+            first = first + decode(y_recv.at[d - 1], 8)
+        total = first.reshape(4, 2, 16, 128)
         for h in range(2):
             encode(total[:, h], z_send.at[h])
         for d in FAR_FIRST:
@@ -371,8 +340,6 @@
             to_all(d).start()
         for d in FAR_FIRST:
             to_z(d).wait_send()
-        for d in (1, 2, 3):
-            to_bx(d).wait_send()
 
     def sent(g, carry):
         for d in (1, 2, 3):
@@ -387,10 +354,6 @@
     lax.fori_loop(0, GROUPS, sent, 0)
     for k in range(3):
         share(k).wait_send()
-    for d in range(1, 8):
-        @pl.when((y + d) % 8 < GROUPS)
-        def _(d=d):
-            to_b(d).wait_send()
     for source, field, base in ((g_hbm, gc, 0), (x_hbm, xc, 17)):
         halo(slab, source, field, base, "wait_send")
     for source, field, base in ((gface, gfr, 0), (xface, xfr, 17)):
@@ -431,16 +394,14 @@
             vm((3, 4, 10, 16, 256), BF16), vm((3, 4, 10, 16, 128), BF16), vm((3, 4, 10, 16, 128), BF16),
             vm((16, 256), BF16), vm((16, 128), BF16), vm((3, 3, 16, 256), BF16), vm((3, 3, 16, 128), BF16),
             vm((3, 3, 16, 128), BF16), vm((8, 2, 16, 256), BF16), vm((8, 16, 256), BF16),
-            vm((GROUPS, 3, 2, 4, 16, 128), F32), vm((2, 4, 16, 128), F32),
-            vm((GROUPS, 3, 7, 16, 128), BF16), vm((GROUPS, 3, 7, 16, 128), BF16), vm((6, 16, 128), F32),
-            vm((GROUPS, 7, 16, 128), BF16), vm((7, 7, 16, 128), BF16),
-            vm((7, 9, 16, 128), BF16), vm((7, 9, 16, 128), BF16),
-            vm((3, 3, 16, 128), BF16), vm((3, 3, 16, 128), BF16),
+            vm((GROUPS, 4, 2, 4, 16, 128), F32),
+            vm((GROUPS, 3, 9, 16, 128), BF16), vm((GROUPS, 3, 9, 16, 128), BF16), vm((8, 16, 128), F32),
+            vm((GROUPS, 9, 16, 128), BF16), vm((7, 9, 16, 128), BF16),
             vm((2, 5, 16, 128), BF16), vm((8, 5, 16, 128), BF16), vm((GROUPS, 5, 16, 128), BF16),
             vm((256, 128), F32), vm((256, 256), F32),
             dma((3,)), dma((34,)), dma((34,)), dma((3,)), dma((3,)),
             dma((GROUPS, 3)), dma((GROUPS, 3)), dma((GROUPS,)), dma((7,)),
-            dma((7,)), dma((7,)), dma((3,)), dma((3,)), dma((7,)), dma((8,)),
+            dma((7,)), dma((8,)),
             dma((7,)), dma((GROUPS,)),
         ],
         compiler_params=pltpu.CompilerParams(

time: 54.1 us -> 54.7 us (1.011)
  the two profiles are of different devices: /device:TPU:8 before, /device:TPU:1 now
where the time goes in v6:
time: 54.7 us; the launch traced here: 54.6 us
  Pallas kernels  51.9 us (95%)
  local copies, waits for them, and re-layouts  1.98 us (4%)
  between operations  0.64 us (1%)
    pallas_call x1, Pallas kernels, per_device(): pl.pallas_call(kernel, out_shape=(jax.ShapeDtypeStruct((2, 8, 16, 128), B...  51.9 us
    unnamed x2, local copies, waits for them, and re-layouts  1.28 us

profile of v6, /device:TPU:1, one launch (start us, length us, event | category | flops | bytes accessed | tf_op | source)
XLA Modules:
  0.0 54.6 jit_solution(11267414094326749313)
XLA Ops:
  0.6 51.9 %shard_map.58 = (bf16[2,8,16,128]{3,2,1,0:T(8,128)(2,1)S(1)}, bf16[2,8,16,256]{3,2,1,0:T(8,128)(2,1)S(1)}, f32[7,4,16,128]{3,2,1,0:T(8,128)S(1)}) custom-call(bf16[2,8,16,256]{3,2,1,0:T(8,128)(2,1)} %bitcast.12, bf16[27,256,128]{2,1,0:T(8,128)(2,1)} %bitcast.11, bf16[2,8,16,128]{3,2,1,0:T(8,128)(2,1)} %bitcast.13), custom_call_target="tpu_custom_call" | custom-call | flops 1400000000 | bytes 3000000 | tf_op jit(solution)/shard_map/pallas_call | solution.py:383
  52.6 0.7 %slice.4 = f32[27,16,128]{2,1,0:T(8,128)} slice(f32[28,16,128]{2,1,0:T(8,128)S(1)} %bitcast.7), slice={[0:27], [0:16], [0:128]} | slice | bytes 442368 | tf_op jit(solution)/shard_map/slice | solution.py:412
  53.3 0.6 %copy.8 = bf16[1,1,2,8,16,128]{5,4,3,2,1,0:T(8,128)(2,1)} copy(bf16[1,1,2,8,16,128]{5,4,3,2,1,0:T(8,128)(2,1)S(1)} %bitcast.9) | data formatting | bytes 131072
  53.9 0.7 %copy.9 = bf16[1,1,2,8,16,256]{5,4,3,2,1,0:T(8,128)(2,1)} copy(bf16[1,1,2,8,16,256]{5,4,3,2,1,0:T(8,128)(2,1)S(1)} %bitcast.8) | data formatting | bytes 262144
